TPU v7x, 256 devices: a whole 4x4x8 slice. The times are simulated.
256 devices in a mesh: tm: 4 (over x), space: 64 (over z, y, core).
Axes of the slice: x: 4, y: 4, z: 8, core: 2. Of those that a mesh axis runs over, the one named last changes fastest.
Arguments:
- init_state: float32 [64, 24576], P(None, 'space'), may hold values from -6 to 6
- guess: float32 [8, 64, 24576], P('tm', None, 'space'), may hold values from -6 to 6
- forcing: float32 [32, 64, 24576], P('tm', None, 'space'), may hold values from -3.5 to 3.5
- volume_block: float32 [64, 64], replicated
- face_blocks: float32 [3, 64, 64], replicated
- elem_scales: float32 [24576], P('space'), may hold values from 0.5 to 1.5
- element_ids: int32 [24576], P('space'), may hold values from 0 to 24575, as said below
- neighbours: int32 [6, 24576], P(None, 'space'), may hold values from 0 to 24575, as said below
- walls: int32 [6, 24576], P(None, 'space'), may hold values from 0 to 1, as said below
Outputs:
- corrected: float32 [8, 64, 24576], P('tm', None, 'space')
Inputs may be any that keep to these rules, and one draw needn't show every extreme that they name: `element_ids`: the device at position d along space holds the elements d * 384 to (d + 1) * 384 - 1, each once, in a drawn order; element number ((z * 8) + y) * 8 + x sits at cell (x, y, z) of the grid. `neighbours`: faces in the order +x, -x, +y, -y, +z, -z; the grid is periodic in x and y; across the two end faces of the third dimension the neighbour is the element itself; a neighbour of an element held on a device is held by that device or is among the 64 lowest numbers of the next device or the 64 highest numbers of the previous one. `walls`: the end faces of the third dimension are closed, and a drawn set of interior faces; a face is closed from both of its sides.
All inputs are finite; a program needn't handle non-finite values.
Results may differ from a plain program's by a relative error of at most 0.0001.
Values sent between devices are 32-bit elements; how exact they have to be, the bound alone decides.
A program may use at most 64 MiB of HBM per device.

v0:
```python
import jax
import jax.numpy as jnp
from jax import lax
from jax.sharding import PartitionSpec as P

GX = 8
GY = 8
COARSEN = 4


def padded(x, sides, width):
    for axis, dim in sides:
        peers, length = (lax.axis_size(axis), x.shape[dim])
        up = [(i, (i + 1) % peers) for i in range(peers - 1)]
        down = [(j, i) for i, j in up]
        last = lax.slice_in_dim(x, length - width, length, axis=dim)
        initial = lax.slice_in_dim(x, 0, width, axis=dim)
        before = lax.ppermute(last, axis, up)
        after = lax.ppermute(initial, axis, down)
        x = jnp.concatenate([before, x, after], axis=dim)
    return x


def passed_along(block, axis, distance):
    devices = range(lax.axis_size(axis))
    route = [(i - distance, i) for i in devices if i - distance in devices]
    return lax.ppermute(block, axis, route)


def make_blocks(face_blocks):
    parts = []
    for m in range(3):
        parts.append(face_blocks[m])
        parts.append(-face_blocks[m].T)
    return jnp.stack(parts)


def apply_grid(extended, table_ext, volume_block, blocks):
    layer = GX * GY
    middle = extended[:, :, layer:-layer]
    above = extended[:, :, 2 * layer :]
    below = extended[:, :, : -2 * layer]
    inner_tab = table_ext[:, layer:-layer]
    count = middle.shape[2]
    cells = jnp.arange(count, dtype=jnp.int32)
    xpos = cells % GX
    ypos = cells // GX % GY
    plus_x = jnp.where(
        xpos == GX - 1, jnp.roll(middle, GX - 1, axis=2), jnp.roll(middle, -1, axis=2)
    )
    minus_x = jnp.where(xpos == 0, jnp.roll(middle, -(GX - 1), axis=2), jnp.roll(middle, 1, axis=2))
    plus_y = jnp.where(
        ypos == GY - 1, jnp.roll(middle, (GY - 1) * GX, axis=2), jnp.roll(middle, -GX, axis=2)
    )
    minus_y = jnp.where(
        ypos == 0, jnp.roll(middle, -(GY - 1) * GX, axis=2), jnp.roll(middle, GX, axis=2)
    )
    near = jnp.stack([plus_x, minus_x, plus_y, minus_y, above, below], axis=2) * inner_tab[:6]
    own = (
        jnp.einsum("ij,cjn->cin", volume_block, middle, precision=lax.Precision.HIGHEST)
        * inner_tab[6]
    )
    return own + jnp.einsum("fij,cjfn->cin", blocks, near, precision=lax.Precision.HIGHEST)


def body(
    init_state,
    guess,
    forcing,
    volume_block,
    face_blocks,
    elem_scales,
    element_ids,
    neighbours,
    walls,
):
    elems = element_ids.shape[0]
    layer = GX * GY
    count = guess.shape[0]
    blocks = make_blocks(face_blocks)
    first_id = lax.axis_index("space") * elems
    local_ids = element_ids - first_id
    inverse = jnp.zeros((elems,), jnp.int32).at[local_ids].set(jnp.arange(elems, dtype=jnp.int32))
    open_grid = jnp.take((1 - walls).astype(jnp.float32), inverse, axis=1)
    scale_grid = jnp.take(elem_scales, inverse, axis=0)
    tables = jnp.concatenate([open_grid, scale_grid[None]], axis=0)
    wide_tables = jnp.pad(tables, ((0, 0), (layer, layer)))

    def rk_step(state, size):

        def operate(value):
            extended = padded(value, (("space", 2),), layer)
            return apply_grid(extended, wide_tables, volume_block, blocks)

        first = size * operate(state)
        second = size * operate(state + 0.5 * first)
        third = size * operate(state + 0.5 * second)
        fourth = size * operate(state + third)
        return state + (first + 2.0 * second + 2.0 * third + fourth) / 6.0

    def sweep(incoming, residual):

        def coarse(carry, term):
            carry = rk_step(carry, float(COARSEN)) + term
            return (carry, carry[0])

        final, errors = lax.scan(coarse, incoming, residual[:, None])
        return errors

    guess_grid = jnp.take(guess, inverse, axis=2)
    forcing_grid = jnp.take(forcing, inverse, axis=2)
    init_grid = jnp.take(init_state, inverse, axis=1)
    previous = passed_along(guess_grid[count - 1 :], "tm", 1)
    first_start = jnp.where(lax.axis_index("tm") == 0, init_grid[None], previous)
    current = jnp.concatenate([first_start, guess_grid[: count - 1]], axis=0)
    sources = forcing_grid.reshape(count, COARSEN, forcing.shape[1], elems)
    for inner in range(COARSEN):
        current = rk_step(current, 1.0) + sources[:, inner]
    residual = current - guess_grid

    def turn(index, incoming):
        errors = sweep(incoming, residual)
        return passed_along(errors[count - 1 :], "tm", 1)

    incoming = lax.fori_loop(0, lax.axis_size("tm") - 1, turn, jnp.zeros_like(residual[:1]))
    errors = sweep(incoming, residual)
    return jnp.take(guess_grid + errors, local_ids, axis=2)


def solution(mesh):
    return jax.shard_map(
        body,
        mesh=mesh,
        in_specs=(
            P(None, "space"),
            P("tm", None, "space"),
            P("tm", None, "space"),
            P(),
            P(),
            P("space"),
            P("space"),
            P(None, "space"),
            P(None, "space"),
        ),
        out_specs=P("tm", None, "space"),
        check_vma=False,
    )
```

profile of v0, /device:TPU:134, one launch (start us, length us, event | category | flops | bytes accessed | tf_op | source)
XLA Modules:
  0.0 639.4 jit_solution(4708283406613387896)
XLA Ops:
  29.3 6.2 collective-permute-done.19
  42.8 5.8 collective-permute-done.21
  56.1 5.6 collective-permute-done.23
  69.0 5.8 collective-permute-done.25
  82.4 5.8 collective-permute-done.27
  95.5 5.8 collective-permute-done.29
  108.6 5.8 collective-permute-done.31
  134.7 5.8 collective-permute-done.35
  147.8 5.8 collective-permute-done.37
  160.9 5.8 collective-permute-done.39
  174.0 5.8 collective-permute-done.41
  200.1 5.8 collective-permute-done.45
  213.2 5.8 collective-permute-done.47
  226.3 5.8 collective-permute-done.49
  233.1 305.9 %while.52 = (s32[]{:T(128)}, f32[1,64,384]{2,1,0:T(8,128)S(1)}, f32[2,64,384]{2,1,0:T(8,128)S(1)}, f32[64,64]{1,0:T(8,128)S(1)}, f32[7,512]{1,0:T(8,128)S(1)}, /...) while((s32[]{:T(128)}, f32[1,64,384]{2,1,0:T(8,128)S(1)}, ...), condition=%wide.region_4.6_spmd, body=%wide.region_1.5_spmd.sunk | while | flops 531058944 | bytes 20754036 | solution.py:125
  233.3 95.2 %while.54 = (s32[]{:T(128)}, f32[1,64,384]{2,1,0:T(8,128)S(1)}, f32[2,64,384]{2,1,0:T(8,128)S(1)}, f32[64,64]{1,0:T(8,128)S(1)}, f32[7,512]{1,0:T(8,128)S(1)}, /...) while((s32[]{:T(128)}, f32[1,64,384]{2,1,0:T(8,128)S(1)}, ...), condition=%wide.region_3.4_spmd, body=%wide.region_2.3_spmd.sunk | while | flops 531058944 | bytes 20164000 | solution.py:107
  250.4 5.7 collective-permute-done.11
  262.6 5.6 collective-permute-done.13
  274.7 5.6 collective-permute-done.15
  298.0 5.7 collective-permute-done.11
  310.2 5.6 collective-permute-done.13
  322.3 5.6 collective-permute-done.15
  335.4 95.2 %while.54 = (s32[]{:T(128)}, f32[1,64,384]{2,1,0:T(8,128)S(1)}, f32[2,64,384]{2,1,0:T(8,128)S(1)}, f32[64,64]{1,0:T(8,128)S(1)}, f32[7,512]{1,0:T(8,128)S(1)}, /...) while((s32[]{:T(128)}, f32[1,64,384]{2,1,0:T(8,128)S(1)}, ...), condition=%wide.region_3.4_spmd, body=%wide.region_2.3_spmd.sunk | while | flops 531058944 | bytes 20164000 | solution.py:107
  352.5 5.7 collective-permute-done.11
  400.1 5.7 collective-permute-done.11
  437.2 95.2 %while.54 = (s32[]{:T(128)}, f32[1,64,384]{2,1,0:T(8,128)S(1)}, f32[2,64,384]{2,1,0:T(8,128)S(1)}, f32[64,64]{1,0:T(8,128)S(1)}, f32[7,512]{1,0:T(8,128)S(1)}, /...) while((s32[]{:T(128)}, f32[1,64,384]{2,1,0:T(8,128)S(1)}, ...), condition=%wide.region_3.4_spmd, body=%wide.region_2.3_spmd.sunk | while | flops 531058944 | bytes 20164000 | solution.py:107
  454.3 5.7 collective-permute-done.11
  501.9 5.7 collective-permute-done.11
  539.0 95.4 %while.53 = (s32[]{:T(128)}, f32[1,64,384]{2,1,0:T(8,128)S(1)}, f32[2,64,384]{2,1,0:T(8,128)S(1)}, f32[64,64]{1,0:T(8,128)S(1)}, f32[7,512]{1,0:T(8,128)S(1)}, /...) while((s32[]{:T(128)}, f32[1,64,384]{2,1,0:T(8,128)S(1)}, ...), condition=%wide.region_6.8_spmd, body=%wide.region_5.7_spmd.sunk | while | flops 531058944 | bytes 20164000 | solution.py:107
  556.2 5.7 collective-permute-done.3
  568.4 5.6 collective-permute-done.5
  603.8 5.7 collective-permute-done.3
  (1126 shorter events, 478.3 us)
Async XLA Ops:
  11.4 8.7 %collective-permute-start.17 = (f32[1,64,384]{2,1,0:T(8,128)}, f32[1,64,384]{2,1,0:T(8,128)}, u32[]{:S(2)}, u32[]{:S(2)}) collective-permute-start(f32[1,64,384]{2,1,0:T(8,128)} %get-tuple-element.901), channel_id=1, source_target_pairs={{0,64},{64,128},{128,192},{1,65},{65,129},{129,193},{2,66},{66,130... | collective-permute-start | bytes 294920 | tf_op jit(solution)/shard_map/ppermute | solution.py:27
  26.6 8.9 %collective-permute-start.19 = (f32[2,64,64]{2,1,0:T(8,128)S(1)}, f32[2,64,64]{2,1,0:T(8,128)S(1)}, u32[]{:S(2)}, u32[]{:S(2)}) collective-permute-start(f32[2,64,64]{2,1,0:T(8,128)S(1)} %get-tuple-element.882), channel_id=1, source_target_pairs={{0,1},{1,2},{2,3},{3,4},{4,5},{5,6},{6,7},{7,8},{8,9},{9,10},{10,1... | collective-permute-start | bytes 98312 | tf_op jit(solution)/shard_map/ppermute | solution.py:18
  39.7 8.9 %collective-permute-start.21 = (f32[2,64,64]{2,1,0:T(8,128)S(1)}, f32[2,64,64]{2,1,0:T(8,128)S(1)}, u32[]{:S(2)}, u32[]{:S(2)}) collective-permute-start(f32[2,64,64]{2,1,0:T(8,128)S(1)} %get-tuple-element.864), channel_id=1, source_target_pairs={{0,1},{1,2},{2,3},{3,4},{4,5},{5,6},{6,7},{7,8},{8,9},{9,10},{10,1... | collective-permute-start | bytes 98312 | tf_op jit(solution)/shard_map/ppermute | solution.py:18
  52.8 8.9 %collective-permute-start.23 = (f32[2,64,64]{2,1,0:T(8,128)S(1)}, f32[2,64,64]{2,1,0:T(8,128)S(1)}, u32[]{:S(2)}, u32[]{:S(2)}) collective-permute-start(f32[2,64,64]{2,1,0:T(8,128)S(1)} %get-tuple-element.846), channel_id=1, source_target_pairs={{0,1},{1,2},{2,3},{3,4},{4,5},{5,6},{6,7},{7,8},{8,9},{9,10},{10,1... | collective-permute-start | bytes 98312 | tf_op jit(solution)/shard_map/ppermute | solution.py:18
  65.8 8.9 %collective-permute-start.25 = (f32[2,64,64]{2,1,0:T(8,128)S(1)}, f32[2,64,64]{2,1,0:T(8,128)S(1)}, u32[]{:S(2)}, u32[]{:S(2)}) collective-permute-start(f32[2,64,64]{2,1,0:T(8,128)S(1)} %get-tuple-element.828), channel_id=1, source_target_pairs={{0,1},{1,2},{2,3},{3,4},{4,5},{5,6},{6,7},{7,8},{8,9},{9,10},{10,1... | collective-permute-start | bytes 98312 | tf_op jit(solution)/shard_map/ppermute | solution.py:18
  79.3 8.9 %collective-permute-start.27 = (f32[2,64,64]{2,1,0:T(8,128)S(1)}, f32[2,64,64]{2,1,0:T(8,128)S(1)}, u32[]{:S(2)}, u32[]{:S(2)}) collective-permute-start(f32[2,64,64]{2,1,0:T(8,128)S(1)} %get-tuple-element.810), channel_id=1, source_target_pairs={{0,1},{1,2},{2,3},{3,4},{4,5},{5,6},{6,7},{7,8},{8,9},{9,10},{10,1... | collective-permute-start | bytes 98312 | tf_op jit(solution)/shard_map/ppermute | solution.py:18
  92.4 8.9 %collective-permute-start.29 = (f32[2,64,64]{2,1,0:T(8,128)S(1)}, f32[2,64,64]{2,1,0:T(8,128)S(1)}, u32[]{:S(2)}, u32[]{:S(2)}) collective-permute-start(f32[2,64,64]{2,1,0:T(8,128)S(1)} %get-tuple-element.792), channel_id=1, source_target_pairs={{0,1},{1,2},{2,3},{3,4},{4,5},{5,6},{6,7},{7,8},{8,9},{9,10},{10,1... | collective-permute-start | bytes 98312 | tf_op jit(solution)/shard_map/ppermute | solution.py:18
  105.4 8.9 %collective-permute-start.31 = (f32[2,64,64]{2,1,0:T(8,128)S(1)}, f32[2,64,64]{2,1,0:T(8,128)S(1)}, u32[]{:S(2)}, u32[]{:S(2)}) collective-permute-start(f32[2,64,64]{2,1,0:T(8,128)S(1)} %get-tuple-element.774), channel_id=1, source_target_pairs={{0,1},{1,2},{2,3},{3,4},{4,5},{5,6},{6,7},{7,8},{8,9},{9,10},{10,1... | collective-permute-start | bytes 98312 | tf_op jit(solution)/shard_map/ppermute | solution.py:18
  118.5 8.9 %collective-permute-start.33 = (f32[2,64,64]{2,1,0:T(8,128)S(1)}, f32[2,64,64]{2,1,0:T(8,128)S(1)}, u32[]{:S(2)}, u32[]{:S(2)}) collective-permute-start(f32[2,64,64]{2,1,0:T(8,128)S(1)} %get-tuple-element.756), channel_id=1, source_target_pairs={{0,1},{1,2},{2,3},{3,4},{4,5},{5,6},{6,7},{7,8},{8,9},{9,10},{10,1... | collective-permute-start | bytes 98312 | tf_op jit(solution)/shard_map/ppermute | solution.py:18
  131.6 8.9 %collective-permute-start.35 = (f32[2,64,64]{2,1,0:T(8,128)S(1)}, f32[2,64,64]{2,1,0:T(8,128)S(1)}, u32[]{:S(2)}, u32[]{:S(2)}) collective-permute-start(f32[2,64,64]{2,1,0:T(8,128)S(1)} %get-tuple-element.738), channel_id=1, source_target_pairs={{0,1},{1,2},{2,3},{3,4},{4,5},{5,6},{6,7},{7,8},{8,9},{9,10},{10,1... | collective-permute-start | bytes 98312 | tf_op jit(solution)/shard_map/ppermute | solution.py:18
  144.7 8.9 %collective-permute-start.37 = (f32[2,64,64]{2,1,0:T(8,128)S(1)}, f32[2,64,64]{2,1,0:T(8,128)S(1)}, u32[]{:S(2)}, u32[]{:S(2)}) collective-permute-start(f32[2,64,64]{2,1,0:T(8,128)S(1)} %get-tuple-element.720), channel_id=1, source_target_pairs={{0,1},{1,2},{2,3},{3,4},{4,5},{5,6},{6,7},{7,8},{8,9},{9,10},{10,1... | collective-permute-start | bytes 98312 | tf_op jit(solution)/shard_map/ppermute | solution.py:18
  157.8 8.9 %collective-permute-start.39 = (f32[2,64,64]{2,1,0:T(8,128)S(1)}, f32[2,64,64]{2,1,0:T(8,128)S(1)}, u32[]{:S(2)}, u32[]{:S(2)}) collective-permute-start(f32[2,64,64]{2,1,0:T(8,128)S(1)} %get-tuple-element.702), channel_id=1, source_target_pairs={{0,1},{1,2},{2,3},{3,4},{4,5},{5,6},{6,7},{7,8},{8,9},{9,10},{10,1... | collective-permute-start | bytes 98312 | tf_op jit(solution)/shard_map/ppermute | solution.py:18
  170.8 8.9 %collective-permute-start.41 = (f32[2,64,64]{2,1,0:T(8,128)S(1)}, f32[2,64,64]{2,1,0:T(8,128)S(1)}, u32[]{:S(2)}, u32[]{:S(2)}) collective-permute-start(f32[2,64,64]{2,1,0:T(8,128)S(1)} %get-tuple-element.684), channel_id=1, source_target_pairs={{0,1},{1,2},{2,3},{3,4},{4,5},{5,6},{6,7},{7,8},{8,9},{9,10},{10,1... | collective-permute-start | bytes 98312 | tf_op jit(solution)/shard_map/ppermute | solution.py:18
  183.9 8.9 %collective-permute-start.43 = (f32[2,64,64]{2,1,0:T(8,128)S(1)}, f32[2,64,64]{2,1,0:T(8,128)S(1)}, u32[]{:S(2)}, u32[]{:S(2)}) collective-permute-start(f32[2,64,64]{2,1,0:T(8,128)S(1)} %get-tuple-element.666), channel_id=1, source_target_pairs={{0,1},{1,2},{2,3},{3,4},{4,5},{5,6},{6,7},{7,8},{8,9},{9,10},{10,1... | collective-permute-start | bytes 98312 | tf_op jit(solution)/shard_map/ppermute | solution.py:18
  197.0 8.9 %collective-permute-start.45 = (f32[2,64,64]{2,1,0:T(8,128)S(1)}, f32[2,64,64]{2,1,0:T(8,128)S(1)}, u32[]{:S(2)}, u32[]{:S(2)}) collective-permute-start(f32[2,64,64]{2,1,0:T(8,128)S(1)} %get-tuple-element.648), channel_id=1, source_target_pairs={{0,1},{1,2},{2,3},{3,4},{4,5},{5,6},{6,7},{7,8},{8,9},{9,10},{10,1... | collective-permute-start | bytes 98312 | tf_op jit(solution)/shard_map/ppermute | solution.py:18
  210.1 8.9 %collective-permute-start.47 = (f32[2,64,64]{2,1,0:T(8,128)S(1)}, f32[2,64,64]{2,1,0:T(8,128)S(1)}, u32[]{:S(2)}, u32[]{:S(2)}) collective-permute-start(f32[2,64,64]{2,1,0:T(8,128)S(1)} %get-tuple-element.630), channel_id=1, source_target_pairs={{0,1},{1,2},{2,3},{3,4},{4,5},{5,6},{6,7},{7,8},{8,9},{9,10},{10,1... | collective-permute-start | bytes 98312 | tf_op jit(solution)/shard_map/ppermute | solution.py:18
  223.2 8.9 %collective-permute-start.49 = (f32[2,64,64]{2,1,0:T(8,128)S(1)}, f32[2,64,64]{2,1,0:T(8,128)S(1)}, u32[]{:S(2)}, u32[]{:S(2)}) collective-permute-start(f32[2,64,64]{2,1,0:T(8,128)S(1)} %get-tuple-element.612), channel_id=1, source_target_pairs={{0,1},{1,2},{2,3},{3,4},{4,5},{5,6},{6,7},{7,8},{8,9},{9,10},{10,1... | collective-permute-start | bytes 98312 | tf_op jit(solution)/shard_map/ppermute | solution.py:18
  235.3 8.6 %collective-permute-start.9 = (f32[1,64,64]{2,1,0:T(8,128)S(1)}, f32[1,64,64]{2,1,0:T(8,128)S(1)}, u32[]{:S(2)}, u32[]{:S(2)}) collective-permute-start(f32[1,64,64]{2,1,0:T(8,128)S(1)} %get-tuple-element.1329), channel_id=1, source_target_pairs={{0,1},{1,2},{2,3},{3,4},{4,5},{5,6},{6,7},{7,8},{8,9},{9,10},{10,1... | collective-permute-start | bytes 49160 | tf_op jit(solution)/shard_map/while/body/eval_jaxpr/while/body/eval_jaxpr/ppermute | solution.py:18
  247.5 8.6 %collective-permute-start.11 = (f32[1,64,64]{2,1,0:T(8,128)S(1)}, f32[1,64,64]{2,1,0:T(8,128)S(1)}, u32[]{:S(2)}, u32[]{:S(2)}) collective-permute-start(f32[1,64,64]{2,1,0:T(8,128)S(1)} %get-tuple-element.1348), channel_id=1, source_target_pairs={{0,1},{1,2},{2,3},{3,4},{4,5},{5,6},{6,7},{7,8},{8,9},{9,10},{10,1... | collective-permute-start | bytes 49160 | tf_op jit(solution)/shard_map/while/body/eval_jaxpr/while/body/eval_jaxpr/ppermute | solution.py:18
  259.6 8.6 %collective-permute-start.13 = (f32[1,64,64]{2,1,0:T(8,128)S(1)}, f32[1,64,64]{2,1,0:T(8,128)S(1)}, u32[]{:S(2)}, u32[]{:S(2)}) collective-permute-start(f32[1,64,64]{2,1,0:T(8,128)S(1)} %get-tuple-element.1367), channel_id=1, source_target_pairs={{0,1},{1,2},{2,3},{3,4},{4,5},{5,6},{6,7},{7,8},{8,9},{9,10},{10,1... | collective-permute-start | bytes 49160 | tf_op jit(solution)/shard_map/while/body/eval_jaxpr/while/body/eval_jaxpr/ppermute | solution.py:18
  271.7 8.6 %collective-permute-start.15 = (f32[1,64,64]{2,1,0:T(8,128)S(1)}, f32[1,64,64]{2,1,0:T(8,128)S(1)}, u32[]{:S(2)}, u32[]{:S(2)}) collective-permute-start(f32[1,64,64]{2,1,0:T(8,128)S(1)} %get-tuple-element.1386), channel_id=1, source_target_pairs={{0,1},{1,2},{2,3},{3,4},{4,5},{5,6},{6,7},{7,8},{8,9},{9,10},{10,1... | collective-permute-start | bytes 49160 | tf_op jit(solution)/shard_map/while/body/eval_jaxpr/while/body/eval_jaxpr/ppermute | solution.py:18
  282.9 8.6 %collective-permute-start.9 = (f32[1,64,64]{2,1,0:T(8,128)S(1)}, f32[1,64,64]{2,1,0:T(8,128)S(1)}, u32[]{:S(2)}, u32[]{:S(2)}) collective-permute-start(f32[1,64,64]{2,1,0:T(8,128)S(1)} %get-tuple-element.1329), channel_id=1, source_target_pairs={{0,1},{1,2},{2,3},{3,4},{4,5},{5,6},{6,7},{7,8},{8,9},{9,10},{10,1... | collective-permute-start | bytes 49160 | tf_op jit(solution)/shard_map/while/body/eval_jaxpr/while/body/eval_jaxpr/ppermute | solution.py:18
  295.1 8.6 %collective-permute-start.11 = (f32[1,64,64]{2,1,0:T(8,128)S(1)}, f32[1,64,64]{2,1,0:T(8,128)S(1)}, u32[]{:S(2)}, u32[]{:S(2)}) collective-permute-start(f32[1,64,64]{2,1,0:T(8,128)S(1)} %get-tuple-element.1348), channel_id=1, source_target_pairs={{0,1},{1,2},{2,3},{3,4},{4,5},{5,6},{6,7},{7,8},{8,9},{9,10},{10,1... | collective-permute-start | bytes 49160 | tf_op jit(solution)/shard_map/while/body/eval_jaxpr/while/body/eval_jaxpr/ppermute | solution.py:18
  307.2 8.6 %collective-permute-start.13 = (f32[1,64,64]{2,1,0:T(8,128)S(1)}, f32[1,64,64]{2,1,0:T(8,128)S(1)}, u32[]{:S(2)}, u32[]{:S(2)}) collective-permute-start(f32[1,64,64]{2,1,0:T(8,128)S(1)} %get-tuple-element.1367), channel_id=1, source_target_pairs={{0,1},{1,2},{2,3},{3,4},{4,5},{5,6},{6,7},{7,8},{8,9},{9,10},{10,1... | collective-permute-start | bytes 49160 | tf_op jit(solution)/shard_map/while/body/eval_jaxpr/while/body/eval_jaxpr/ppermute | solution.py:18
  319.4 8.6 %collective-permute-start.15 = (f32[1,64,64]{2,1,0:T(8,128)S(1)}, f32[1,64,64]{2,1,0:T(8,128)S(1)}, u32[]{:S(2)}, u32[]{:S(2)}) collective-permute-start(f32[1,64,64]{2,1,0:T(8,128)S(1)} %get-tuple-element.1386), channel_id=1, source_target_pairs={{0,1},{1,2},{2,3},{3,4},{4,5},{5,6},{6,7},{7,8},{8,9},{9,10},{10,1... | collective-permute-start | bytes 49160 | tf_op jit(solution)/shard_map/while/body/eval_jaxpr/while/body/eval_jaxpr/ppermute | solution.py:18
  337.4 8.6 %collective-permute-start.9 = (f32[1,64,64]{2,1,0:T(8,128)S(1)}, f32[1,64,64]{2,1,0:T(8,128)S(1)}, u32[]{:S(2)}, u32[]{:S(2)}) collective-permute-start(f32[1,64,64]{2,1,0:T(8,128)S(1)} %get-tuple-element.1329), channel_id=1, source_target_pairs={{0,1},{1,2},{2,3},{3,4},{4,5},{5,6},{6,7},{7,8},{8,9},{9,10},{10,1... | collective-permute-start | bytes 49160 | tf_op jit(solution)/shard_map/while/body/eval_jaxpr/while/body/eval_jaxpr/ppermute | solution.py:18
  349.6 8.6 %collective-permute-start.11 = (f32[1,64,64]{2,1,0:T(8,128)S(1)}, f32[1,64,64]{2,1,0:T(8,128)S(1)}, u32[]{:S(2)}, u32[]{:S(2)}) collective-permute-start(f32[1,64,64]{2,1,0:T(8,128)S(1)} %get-tuple-element.1348), channel_id=1, source_target_pairs={{0,1},{1,2},{2,3},{3,4},{4,5},{5,6},{6,7},{7,8},{8,9},{9,10},{10,1... | collective-permute-start | bytes 49160 | tf_op jit(solution)/shard_map/while/body/eval_jaxpr/while/body/eval_jaxpr/ppermute | solution.py:18
  361.7 8.6 %collective-permute-start.13 = (f32[1,64,64]{2,1,0:T(8,128)S(1)}, f32[1,64,64]{2,1,0:T(8,128)S(1)}, u32[]{:S(2)}, u32[]{:S(2)}) collective-permute-start(f32[1,64,64]{2,1,0:T(8,128)S(1)} %get-tuple-element.1367), channel_id=1, source_target_pairs={{0,1},{1,2},{2,3},{3,4},{4,5},{5,6},{6,7},{7,8},{8,9},{9,10},{10,1... | collective-permute-start | bytes 49160 | tf_op jit(solution)/shard_map/while/body/eval_jaxpr/while/body/eval_jaxpr/ppermute | solution.py:18
  373.8 8.6 %collective-permute-start.15 = (f32[1,64,64]{2,1,0:T(8,128)S(1)}, f32[1,64,64]{2,1,0:T(8,128)S(1)}, u32[]{:S(2)}, u32[]{:S(2)}) collective-permute-start(f32[1,64,64]{2,1,0:T(8,128)S(1)} %get-tuple-element.1386), channel_id=1, source_target_pairs={{0,1},{1,2},{2,3},{3,4},{4,5},{5,6},{6,7},{7,8},{8,9},{9,10},{10,1... | collective-permute-start | bytes 49160 | tf_op jit(solution)/shard_map/while/body/eval_jaxpr/while/body/eval_jaxpr/ppermute | solution.py:18
  385.1 8.6 %collective-permute-start.9 = (f32[1,64,64]{2,1,0:T(8,128)S(1)}, f32[1,64,64]{2,1,0:T(8,128)S(1)}, u32[]{:S(2)}, u32[]{:S(2)}) collective-permute-start(f32[1,64,64]{2,1,0:T(8,128)S(1)} %get-tuple-element.1329), channel_id=1, source_target_pairs={{0,1},{1,2},{2,3},{3,4},{4,5},{5,6},{6,7},{7,8},{8,9},{9,10},{10,1... | collective-permute-start | bytes 49160 | tf_op jit(solution)/shard_map/while/body/eval_jaxpr/while/body/eval_jaxpr/ppermute | solution.py:18
  565.4 8.6 %collective-permute-start.5 = (f32[1,64,64]{2,1,0:T(8,128)S(1)}, f32[1,64,64]{2,1,0:T(8,128)S(1)}, u32[]{:S(2)}, u32[]{:S(2)}) collective-permute-start(f32[1,64,64]{2,1,0:T(8,128)S(1)} %get-tuple-element.1280), channel_id=1, source_target_pairs={{0,1},{1,2},{2,3},{3,4},{4,5},{5,6},{6,7},{7,8},{8,9},{9,10},{10,1... | collective-permute-start | bytes 49160 | tf_op jit(solution)/shard_map/while/body/eval_jaxpr/ppermute | solution.py:18
  600.9 8.6 %collective-permute-start.3 = (f32[1,64,64]{2,1,0:T(8,128)S(1)}, f32[1,64,64]{2,1,0:T(8,128)S(1)}, u32[]{:S(2)}, u32[]{:S(2)}) collective-permute-start(f32[1,64,64]{2,1,0:T(8,128)S(1)} %get-tuple-element.1261), channel_id=1, source_target_pairs={{0,1},{1,2},{2,3},{3,4},{4,5},{5,6},{6,7},{7,8},{8,9},{9,10},{10,1... | collective-permute-start | bytes 49160 | tf_op jit(solution)/shard_map/while/body/eval_jaxpr/ppermute | solution.py:18
  (86 other events, 971.1 us)
where the time goes:
time: 651 us; the launch traced here: 639 us
  waiting for transfers between devices  279 us (43%)
  starting transfers between devices  215 us (33%)
  local copies, waits for them, and re-layouts  58.4 us (9%)
  matrix products  43.7 us (7%)
  other arithmetic  36.5 us (6%)
    ppermute x48, waiting for transfers between devices, padded(): before = lax.ppermute(last, axis, up)  263 us
    ppermute x48, starting transfers between devices, padded(): before = lax.ppermute(last, axis, up)  115 us
    ppermute x48, starting transfers between devices, padded(): after = lax.ppermute(initial, axis, down)  94.9 us
    dot_general x48, matrix products, apply_grid(): jnp.einsum('fij,cjfn->cin', blocks, near, precision=lax.Precision.HIGHEST)  30.8 us
    ppermute x4, waiting for transfers between devices, passed_along(): return lax.ppermute(block, axis, route)  16 us
    while x160, other arithmetic  15.7 us
  transfers between devices with their start and end apart: 100, of which 51 were waited for; matrix products, arithmetic and copies ran while one was open for 7% of the time, Pallas kernels for 0%

commit v1 on v0

v1 whole, which is shorter than its diff:
```python
import functools
import jax
import jax.numpy as jnp
from jax import lax
from jax.experimental import pallas as pl
from jax.experimental.pallas import tpu as pltpu
from jax.sharding import PartitionSpec as P

GX = 8
LAYER = 64
DOF = 64
COARSEN = 4
HALO = 4
MESH = pl.DeviceIdType.MESH
F32 = jnp.float32
BF16 = jnp.bfloat16


def halves(x):
    hi = x.astype(BF16)
    return hi, (x - hi.astype(F32)).astype(BF16)


def thirds(x):
    hi = x.astype(BF16)
    rest = x - hi.astype(F32)
    mid = rest.astype(BF16)
    return hi, mid, (rest - mid.astype(F32)).astype(BF16)


def times_t(a, b):
    return lax.dot_general(a, b, (((1,), (1,)), ((), ())), preferred_element_type=F32)


def select_rows(perm, values):
    hi, mid, lo = thirds(values)
    return (times_t(perm, hi) + times_t(perm, mid)) + times_t(perm, lo)


def left_lanes(rows):
    return lax.broadcasted_iota(jnp.int32, (rows, 2 * DOF), 1) < DOF


def swapped(x):
    return pltpu.roll(x, DOF, 1)


def doubled(packed):
    left = left_lanes(packed.shape[0])
    other = swapped(packed)
    return jnp.where(left, packed, other), jnp.where(left, other, packed)


def one_hot(ids_row, first, rows):
    cells = lax.broadcasted_iota(jnp.int32, (rows, ids_row.shape[1]), 0) + first
    return (ids_row == cells).astype(F32).astype(BF16)


def table_of(perm, faces):
    flags = jnp.concatenate(
        [jnp.broadcast_to(faces[f : f + 1], (DOF, faces.shape[1])) for f in range(6)], axis=0
    )
    scale = jnp.broadcast_to(faces[6:7], (2 * DOF, faces.shape[1]))
    return times_t(perm, flags.astype(BF16)), select_rows(perm, scale)


def kernel(
    layers,
    count,
    init_ref,
    guess_ref,
    forcing_ref,
    volume_ref,
    faces_ref,
    scales_ref,
    ids_ref,
    walls_ref,
    out_ref,
    weights,
    table,
    perm_ref,
    sources,
    guess_grid,
    state,
    ext_a,
    ext_b,
    split_a,
    split_b,
    prod_a,
    prod_b,
    errors,
    faces_out,
    faces_in,
    guess_in,
    fine_out,
    fine_in,
    coarse_out,
    coarse_in,
    res_in,
    faces_send,
    faces_recv,
    guess_send,
    guess_recv,
    fine_send,
    fine_recv,
    coarse_send,
    coarse_recv,
    res_send,
    res_recv,
):
    times = lax.axis_size("tm")
    spaces = lax.axis_size("space")
    tme = lax.axis_index("tm")
    sme = lax.axis_index("space")
    up = lax.rem(sme + 1, spaces)
    down = lax.rem(sme + spaces - 1, spaces)
    own = layers * LAYER
    ext = layers + 2 * HALO

    barrier = pltpu.get_barrier_semaphore()
    pl.semaphore_signal(barrier, inc=1, device_id=(tme, up), device_id_type=MESH)
    pl.semaphore_signal(barrier, inc=1, device_id=(tme, down), device_id_type=MESH)
    for step in range(1, times):
        pl.semaphore_signal(
            barrier, inc=1, device_id=(lax.rem(tme + step, times), sme), device_id_type=MESH
        )

    local = ids_ref[...] - sme * own
    faces_out[0:6, :] = (1 - walls_ref[...]).astype(F32)
    faces_out[6:7, :] = scales_ref[...]
    faces_out[7:8, :] = local.astype(F32)

    pl.semaphore_wait(barrier, 2 + times - 1)

    def sends(source_up, source_down, target, send, recv):
        return (
            pltpu.make_async_remote_copy(
                src_ref=source_up,
                dst_ref=target(0),
                send_sem=send(0),
                recv_sem=recv(0),
                device_id=(tme, up),
                device_id_type=MESH,
            ),
            pltpu.make_async_remote_copy(
                src_ref=source_down,
                dst_ref=target(1),
                send_sem=send(1),
                recv_sem=recv(1),
                device_id=(tme, down),
                device_id_type=MESH,
            ),
        )

    guess_copy = pltpu.make_async_remote_copy(
        src_ref=guess_ref.at[count - 1],
        dst_ref=guess_in,
        send_sem=guess_send,
        recv_sem=guess_recv,
        device_id=(lax.rem(tme + 1, times), sme),
        device_id_type=MESH,
    )
    guess_copy.start()
    faces_copies = sends(
        faces_out,
        faces_out,
        lambda i: faces_in.at[i],
        lambda i: faces_send.at[i],
        lambda i: faces_recv.at[i],
    )
    for copy in faces_copies:
        copy.start()

    perm = one_hot(local, 0, own)
    perm_ref[...] = perm
    guess_grid[...] = select_rows(
        perm, jnp.concatenate([guess_ref[0], guess_ref[1]], axis=0)
    )
    blocks = []
    for m in range(3):
        face = faces_ref[m]
        blocks.append(face.T)
        blocks.append(-face)
    blocks.append(volume_ref[...].T)
    blocks.append(jnp.zeros((DOF, DOF), F32))
    for pair in range(4):
        high, low = halves(jnp.concatenate(blocks[2 * pair : 2 * pair + 2], axis=1))
        weights[:, pair * 2 * DOF : (pair + 1) * 2 * DOF] = jnp.concatenate(
            [high, high, low, low], axis=0
        )
    inner_flags, inner_scale = table_of(perm, faces_out[...])
    table[3 * LAYER : 3 * LAYER + own, 0 : 6 * DOF] = inner_flags
    table[3 * LAYER : 3 * LAYER + own, 6 * DOF : 8 * DOF] = inner_scale

    guess_copy.wait()
    first = jnp.where(tme == 0, init_ref[...], guess_in[...])
    state[...] = select_rows(perm, jnp.concatenate([first, guess_ref[0]], axis=0))

    def product(split, prod, low, high):
        rows = split[low * LAYER : high * LAYER, :]
        wide = jnp.concatenate([rows, rows], axis=1)
        prod[low * LAYER : high * LAYER, 4 * DOF :] = jnp.dot(
            wide, weights[:, 4 * DOF :], preferred_element_type=F32
        )
        prod[(low + 1) * LAYER : (high - 1) * LAYER, : 4 * DOF] = jnp.dot(
            wide[LAYER:-LAYER], weights[:, : 4 * DOF], preferred_element_type=F32
        )

    def combined(prod, layer):
        base = layer * LAYER
        left = left_lanes(LAYER)
        left3 = left.reshape(LAYER // GX, GX, 2 * DOF)
        px = prod[base : base + LAYER, 0 : 2 * DOF].reshape(LAYER // GX, GX, 2 * DOF)
        xs = jnp.where(left3, pltpu.roll(px, GX - 1, 1), pltpu.roll(px, 1, 1))
        py = prod[base : base + LAYER, 2 * DOF : 4 * DOF].reshape(LAYER // GX, GX, 2 * DOF)
        ys = jnp.where(
            left3,
            jnp.concatenate([py[1:], py[:1]], axis=0),
            jnp.concatenate([py[-1:], py[:-1]], axis=0),
        )
        zs = jnp.where(
            left,
            prod[base + LAYER : base + 2 * LAYER, 4 * DOF : 6 * DOF],
            prod[base - LAYER : base, 4 * DOF : 6 * DOF],
        )
        own_term = prod[base : base + LAYER, 6 * DOF : 8 * DOF]
        tb = base - LAYER
        total = (
            table[tb : tb + LAYER, 0 : 2 * DOF] * xs.reshape(LAYER, 2 * DOF)
            + table[tb : tb + LAYER, 2 * DOF : 4 * DOF] * ys.reshape(LAYER, 2 * DOF)
        ) + (
            table[tb : tb + LAYER, 4 * DOF : 6 * DOF] * zs
            + table[tb : tb + LAYER, 6 * DOF : 8 * DOF] * own_term
        )
        return total + swapped(total)

    def store_split(split, layer, value):
        low = value - value.astype(BF16).astype(F32)
        split[layer * LAYER : (layer + 1) * LAYER, :] = jnp.where(
            left_lanes(LAYER), value, low
        ).astype(BF16)

    def rk_steps(fields, size, finish):
        for x, split, prod in fields:
            for layer in range(ext):
                store_split(split, layer, x[layer * LAYER : (layer + 1) * LAYER, :])
        for stage in range(4):
            low, high = stage, ext - stage
            factor = size / (4 - stage)
            for x, split, prod in fields:
                product(split, prod, low, high)
            for index, (x, split, prod) in enumerate(fields):
                for layer in range(low + 1, high - 1):
                    value = x[layer * LAYER : (layer + 1) * LAYER, :] + factor * combined(prod, layer)
                    if stage < 3:
                        store_split(split, layer, value)
                    else:
                        finish(index, layer - HALO, value)

    def fine(inner, carry):
        parity = lax.rem(inner, 2)
        fine_out[...] = state[...]
        copies = sends(
            fine_out.at[pl.ds(own - HALO * LAYER, HALO * LAYER)],
            fine_out.at[pl.ds(0, HALO * LAYER)],
            lambda i: fine_in.at[parity, i],
            lambda i: fine_send.at[i],
            lambda i: fine_recv.at[parity, i],
        )
        for copy in copies:
            copy.start()

        @pl.when(inner == 0)
        def _():
            for step in range(COARSEN):
                pieces = jnp.concatenate([forcing_ref[step], forcing_ref[COARSEN + step]], axis=0)
                sources[step] = select_rows(perm_ref[...], pieces)
            for copy in faces_copies:
                copy.wait()
            for side in range(2):
                faces = faces_in[side]
                begin = own - 3 * LAYER if side == 0 else 0
                place = 0 if side == 0 else 3 * LAYER + own
                other = one_hot(faces[7:8].astype(jnp.int32), begin, 3 * LAYER)
                flags, scale = table_of(other, faces)
                table[place : place + 3 * LAYER, 0 : 6 * DOF] = flags
                table[place : place + 3 * LAYER, 6 * DOF : 8 * DOF] = scale

        def spread(layer, packed):
            one, two = doubled(packed)
            ext_a[layer * LAYER : (layer + 1) * LAYER, :] = one
            ext_b[layer * LAYER : (layer + 1) * LAYER, :] = two

        for layer in range(layers):
            spread(HALO + layer, state[layer * LAYER : (layer + 1) * LAYER, :])
        for copy in copies:
            copy.wait()
        for layer in range(HALO):
            rows = pl.ds(layer * LAYER, LAYER)
            spread(layer, fine_in[parity, 0, rows, :])
            spread(HALO + layers + layer, fine_in[parity, 1, rows, :])

        def finish(index, layer, value):
            rows = pl.ds(layer * LAYER, LAYER)
            if index == 0:
                state[rows, :] = value
            else:
                state[rows, :] = jnp.where(left_lanes(LAYER), state[rows, :], value) + sources[inner, rows, :]

        rk_steps(((ext_a, split_a, prod_a), (ext_b, split_b, prod_b)), 1.0, finish)
        return carry

    lax.fori_loop(0, COARSEN, fine, 0)

    res_in[tme] = state[...] - guess_grid[...]
    res_copies = []
    for step in range(1, times):
        target = lax.rem(tme + step, times)
        res_copies.append(
            pltpu.make_async_remote_copy(
                src_ref=res_in.at[tme],
                dst_ref=res_in.at[tme],
                send_sem=res_send.at[step],
                recv_sem=res_recv.at[step],
                device_id=(target, sme),
                device_id_type=MESH,
            )
        )
    for copy in res_copies:
        copy.start()
    for copy in res_copies:
        copy.wait()

    points = times * count
    for block in range(times):
        one, two = doubled(res_in[block])
        errors[2 * block] = one
        errors[2 * block + 1] = two

    def coarse(point, carry):
        parity = lax.rem(point, 2)
        half = HALO // 2
        for layer in range(half):
            rows = pl.ds(layer * LAYER, LAYER)
            left = left_lanes(LAYER)
            top = (layers - HALO + layer) * LAYER
            coarse_out[0, rows, :] = jnp.where(
                left,
                errors[point - 1, pl.ds(top, LAYER), :],
                errors[point - 1, pl.ds(top + half * LAYER, LAYER), :],
            )
            coarse_out[1, rows, :] = jnp.where(
                left,
                errors[point - 1, pl.ds(layer * LAYER, LAYER), :],
                errors[point - 1, pl.ds((layer + half) * LAYER, LAYER), :],
            )
        copies = sends(
            coarse_out.at[0],
            coarse_out.at[1],
            lambda i: coarse_in.at[parity, i],
            lambda i: coarse_send.at[i],
            lambda i: coarse_recv.at[parity, i],
        )
        for copy in copies:
            copy.start()
        ext_a[HALO * LAYER : HALO * LAYER + own, :] = errors[point - 1]
        for copy in copies:
            copy.wait()
        for side in range(2):
            base = 0 if side == 0 else HALO + layers
            for layer in range(half):
                one, two = doubled(coarse_in[parity, side, pl.ds(layer * LAYER, LAYER), :])
                ext_a[pl.ds((base + layer) * LAYER, LAYER), :] = one
                ext_a[pl.ds((base + half + layer) * LAYER, LAYER), :] = two

        def finish(index, layer, value):
            rows = pl.ds(layer * LAYER, LAYER)
            errors[point, rows, :] = errors[point, rows, :] + value

        rk_steps(((ext_a, split_a, prod_a),), float(COARSEN), finish)
        return carry

    lax.fori_loop(1, points, coarse, 0)

    packed = jnp.where(left_lanes(own), errors[count * tme], errors[count * tme + 1])
    parts = [
        lax.dot_general(part, perm_ref[...], (((0,), (0,)), ((), ())), preferred_element_type=F32)
        for part in thirds(packed)
    ]
    result = (parts[0] + parts[1]) + parts[2]
    out_ref[0] = result[:DOF]
    out_ref[1] = result[DOF:]


def body(init_state, guess, forcing, volume_block, face_blocks, elem_scales, element_ids, neighbours, walls):
    own = element_ids.shape[0]
    layers = own // LAYER
    count = guess.shape[0]
    times = lax.axis_size("tm")
    ext = (layers + 2 * HALO) * LAYER
    wide = 2 * DOF
    vmem = pl.BlockSpec(memory_space=pltpu.VMEM)
    dma = pltpu.SemaphoreType.DMA
    errors = pl.pallas_call(
        functools.partial(kernel, layers, count),
        out_shape=jax.ShapeDtypeStruct(guess.shape, F32),
        in_specs=[vmem] * 8,
        out_specs=vmem,
        scratch_shapes=[
            pltpu.VMEM((4 * DOF, 8 * DOF), BF16),
            pltpu.VMEM((own + 6 * LAYER, 8 * DOF), F32),
            pltpu.VMEM((own, own), BF16),
            pltpu.VMEM((COARSEN, own, wide), F32),
            pltpu.VMEM((own, wide), F32),
            pltpu.VMEM((own, wide), F32),
            pltpu.VMEM((ext, wide), F32),
            pltpu.VMEM((ext, wide), F32),
            pltpu.VMEM((ext, wide), BF16),
            pltpu.VMEM((ext, wide), BF16),
            pltpu.VMEM((ext, 8 * DOF), F32),
            pltpu.VMEM((ext, 8 * DOF), F32),
            pltpu.VMEM((times * count, own, wide), F32),
            pltpu.VMEM((8, own), F32),
            pltpu.VMEM((2, 8, own), F32),
            pltpu.VMEM((DOF, own), F32),
            pltpu.VMEM((own, wide), F32),
            pltpu.VMEM((2, 2, HALO * LAYER, wide), F32),
            pltpu.VMEM((2, HALO // 2 * LAYER, wide), F32),
            pltpu.VMEM((2, 2, HALO // 2 * LAYER, wide), F32),
            pltpu.VMEM((times, own, wide), F32),
            dma((2,)),
            dma((2,)),
            dma,
            dma,
            dma((2,)),
            dma((2, 2)),
            dma((2,)),
            dma((2, 2)),
            dma((times,)),
            dma((times,)),
        ],
        compiler_params=pltpu.CompilerParams(
            collective_id=0, has_side_effects=True, vmem_limit_bytes=48 * 1024 * 1024
        ),
    )(
        init_state,
        guess,
        forcing,
        volume_block,
        face_blocks,
        elem_scales.reshape(1, own),
        element_ids.reshape(1, own),
        walls,
    )
    return guess + errors


def solution(mesh):
    return jax.shard_map(
        body,
        mesh=mesh,
        in_specs=(
            P(None, "space"),
            P("tm", None, "space"),
            P("tm", None, "space"),
            P(),
            P(),
            P("space"),
            P("space"),
            P(None, "space"),
            P(None, "space"),
        ),
        out_specs=P("tm", None, "space"),
        check_vma=False,
    )
```

time: 651 us -> 96.9 us (0.15)
  the two profiles are of different devices: /device:TPU:134 before, /device:TPU:4 now
where the time goes in v1:
time: 96.9 us; the launch traced here: 96.6 us
  Pallas kernels  89.9 us (93%)
  local copies, waits for them, and re-layouts  6.01 us (6%)
    pallas_call x1, Pallas kernels, body(): pl.pallas_call(functools.partial(kernel, layers, count), out_shape=jax.Sh...  89.9 us
    unnamed x14, local copies, waits for them, and re-layouts  5.31 us

profile of v1, /device:TPU:4, one launch (start us, length us, event | category | flops | bytes accessed | tf_op | source)
XLA Modules:
  0.0 96.6 jit_solution(10438991564467783677)
XLA Ops:
  0.0 0.0 copy-start.6
  0.0 0.7 reshape.6.scales_ref
  0.7 0.0 copy-done.6
  0.7 0.0 copy-start
  0.7 1.1 %copy-done = f32[8,64,384]{2,1,0:T(8,128)S(1)} copy-done((f32[8,64,384]{2,1,0:T(8,128)S(1)}, f32[8,64,384]{2,1,0:T(8,128)}, u32[]{:S(2)}) %copy-start) | copy-done | bytes 786456
  1.8 0.0 copy-start.1
  1.8 0.9 copy-done.1
  2.8 0.0 copy-start.2
  2.8 0.9 copy-done.2
  3.7 0.0 copy-start.3
  3.7 0.9 copy-done.3
  4.6 0.0 copy-start.4
  4.6 0.8 copy-done.4
  5.3 0.0 copy-start.5
  5.3 0.7 copy-done.5
  6.0 89.9 %shard_map.82 = f32[2,64,384]{2,1,0:T(8,128)S(1)} custom-call(f32[64,384]{1,0:T(8,128)S(1)} %copy-done.2, f32[2,64,384]{2,1,0:T(8,128)S(1)} %copy-done.1, f32[8,64,384]{2,1,0:T(8,128)S(1)} %copy-done, f32[64,64]{1,0:T(8,128)S(1)} %copy-done.4, f32[3,64,64]{2,1,0:T(8,128)S(1)} %copy-done.3, f32[1,384]{1,0:T(1,128)S(1)} %reshape.6.scales_ref, ...), custom_call_target="tpu_custom_call" | custom-call | tf_op jit(solution)/shard_map/pallas_call | solution.py:404
  95.9 0.7 add.3
  (1 shorter events, 0.0 us)
Async XLA Ops:
  0.0 0.7 copy-start.6
  0.7 1.1 %copy-start = (f32[8,64,384]{2,1,0:T(8,128)S(1)}, f32[8,64,384]{2,1,0:T(8,128)}, u32[]{:S(2)}) copy-start(f32[8,64,384]{2,1,0:T(8,128)} %forcing_ref.1) | copy-start | bytes 2359300
  1.8 0.9 copy-start.1
  2.8 0.9 copy-start.2
  3.7 0.9 copy-start.3
  4.6 0.8 copy-start.4
  5.3 0.7 copy-start.5

commit v2 on v1

v2 whole, which is shorter than its diff:
```python
import functools
import jax
import jax.numpy as jnp
from jax import lax
from jax.experimental import pallas as pl
from jax.experimental.pallas import tpu as pltpu
from jax.sharding import PartitionSpec as P

GX = 8
LAYER = 64
DOF = 64
COARSEN = 4
HALO = 4
MESH = pl.DeviceIdType.MESH
F32 = jnp.float32
BF16 = jnp.bfloat16


def halves(x):
    hi = x.astype(BF16)
    return hi, (x - hi.astype(F32)).astype(BF16)


def thirds(x):
    hi = x.astype(BF16)
    rest = x - hi.astype(F32)
    mid = rest.astype(BF16)
    return hi, mid, (rest - mid.astype(F32)).astype(BF16)


def times_t(a, b):
    return lax.dot_general(a, b, (((1,), (1,)), ((), ())), preferred_element_type=F32)


def select_rows(perm, values):
    hi, mid, lo = thirds(values)
    return (times_t(perm, hi) + times_t(perm, mid)) + times_t(perm, lo)


def left_lanes(rows):
    return lax.broadcasted_iota(jnp.int32, (rows, 2 * DOF), 1) < DOF


def swapped(x):
    return pltpu.roll(x, DOF, 1)


def doubled(packed):
    left = left_lanes(packed.shape[0])
    other = swapped(packed)
    return jnp.where(left, packed, other), jnp.where(left, other, packed)


def one_hot(ids_row, first, rows):
    cells = lax.broadcasted_iota(jnp.int32, (rows, ids_row.shape[1]), 0) + first
    return (ids_row == cells).astype(F32).astype(BF16)


def table_of(perm, faces):
    flags = jnp.concatenate(
        [jnp.broadcast_to(faces[f : f + 1], (DOF, faces.shape[1])) for f in range(6)], axis=0
    )
    scale = jnp.broadcast_to(faces[6:7], (2 * DOF, faces.shape[1]))
    return times_t(perm, flags.astype(BF16)), select_rows(perm, scale)


def kernel(
    layers,
    count,
    init_hbm,
    guess_hbm,
    forcing_hbm,
    volume_hbm,
    faces_hbm,
    scales_hbm,
    ids_hbm,
    walls_hbm,
    out_ref,
    init_ref,
    guess_ref,
    forcing_ref,
    volume_ref,
    faces_ref,
    scales_ref,
    ids_ref,
    walls_ref,
    weights,
    table,
    perm_ref,
    sources,
    guess_grid,
    ext_a,
    ext_b,
    split,
    prod,
    errors,
    tables_out,
    tables_in,
    guess_in,
    fine_out,
    fine_in,
    piece_out,
    piece_in,
    edge_out,
    edge_in,
    res_out,
    res_in,
    load_sem,
    tables_send,
    tables_recv,
    guess_send,
    guess_recv,
    fine_send,
    fine_recv,
    piece_send,
    piece_recv,
    edge_send,
    edge_recv,
    res_send,
    res_recv,
):
    times = lax.axis_size("tm")
    spaces = lax.axis_size("space")
    tme = lax.axis_index("tm")
    sme = lax.axis_index("space")
    own = layers * LAYER
    off = 2 * HALO
    end = off + layers
    around = [lax.rem(sme + spaces + step, spaces) for step in (1, -1, 2, -2)]

    pairs = (
        (ids_hbm, ids_ref),
        (walls_hbm, walls_ref),
        (scales_hbm, scales_ref),
        (guess_hbm, guess_ref),
        (faces_hbm, faces_ref),
        (volume_hbm, volume_ref),
        (init_hbm, init_ref),
        (forcing_hbm, forcing_ref),
    )
    loads = [pltpu.make_async_copy(a, b, load_sem.at[i]) for i, (a, b) in enumerate(pairs)]
    for copy in loads:
        copy.start()

    barrier = pltpu.get_barrier_semaphore()
    for device in around:
        pl.semaphore_signal(barrier, inc=1, device_id=(tme, device), device_id_type=MESH)
    for step in range(1, times):
        pl.semaphore_signal(
            barrier, inc=1, device_id=(lax.rem(tme + step, times), sme), device_id_type=MESH
        )

    def rows_of(layer, number=1):
        return pl.ds(layer * LAYER, number * LAYER)

    for copy in loads[:3]:
        copy.wait()
    local = ids_ref[...] - sme * own
    tables_out[0:6, :] = (1 - walls_ref[...]).astype(F32)
    tables_out[6:7, :] = scales_ref[...]
    tables_out[7:8, :] = local.astype(F32)
    perm = one_hot(local, 0, own)
    perm_ref[...] = perm

    def permuted_pair(first, second):
        return doubled(select_rows(perm_ref[...], jnp.concatenate([first, second], axis=0)))

    loads[3].wait()
    one, two = permuted_pair(guess_ref[0], guess_ref[1])
    guess_grid[0] = one
    guess_grid[1] = two
    ext_b[rows_of(off, layers), :] = one

    def pack(target, source, first, number):
        for layer in range(number):
            target[layer * LAYER : (layer + 1) * LAYER, :] = jnp.where(
                left_lanes(LAYER),
                source[rows_of(first + layer), :],
                source[rows_of(first + number + layer), :],
            )

    def unpack(source, target, first, number):
        for layer in range(number):
            one, two = doubled(source[layer * LAYER : (layer + 1) * LAYER, :])
            target[rows_of(first + layer), :] = one
            target[rows_of(first + number + layer), :] = two

    half = HALO // 2

    def fine_copies(point, step):
        return [
            pltpu.make_async_remote_copy(
                src_ref=fine_out.at[point, step, side],
                dst_ref=fine_in.at[point, step, side],
                send_sem=fine_send.at[point, step, side],
                recv_sem=fine_recv.at[point, step, side],
                device_id=(tme, around[side]),
                device_id_type=MESH,
            )
            for side in range(2)
        ]

    def send_fine(point, step, ext):
        pack(fine_out.at[point, step, 0], ext, end - HALO, half)
        pack(fine_out.at[point, step, 1], ext, off, half)
        for copy in fine_copies(point, step):
            copy.start()

    def receive_fine(point, step, ext):
        for side, copy in enumerate(fine_copies(point, step)):
            copy.wait_recv()
            unpack(fine_in.at[point, step, side], ext, off - HALO if side == 0 else end, half)

    pl.semaphore_wait(barrier, 4 + times - 1)

    guess_copy = pltpu.make_async_remote_copy(
        src_ref=guess_ref.at[count - 1],
        dst_ref=guess_in,
        send_sem=guess_send,
        recv_sem=guess_recv,
        device_id=(lax.rem(tme + 1, times), sme),
        device_id_type=MESH,
    )
    guess_copy.start()
    tables_copies = [
        pltpu.make_async_remote_copy(
            src_ref=tables_out,
            dst_ref=tables_in.at[slot],
            send_sem=tables_send.at[slot],
            recv_sem=tables_recv.at[slot],
            device_id=(tme, around[slot]),
            device_id_type=MESH,
        )
        for slot in range(4)
    ]
    for copy in tables_copies:
        copy.start()
    send_fine(1, 0, ext_b)

    for copy in loads[4:7]:
        copy.wait()

    @pl.when(tme == 0)
    def _():
        one, _ = permuted_pair(init_ref[...], init_ref[...])
        ext_a[rows_of(off, layers), :] = one
        send_fine(0, 0, ext_a)

    blocks = []
    for m in range(3):
        face = faces_ref[m]
        blocks.append(face.T)
        blocks.append(-face)
    blocks.append(volume_ref[...].T)
    blocks.append(jnp.zeros((DOF, DOF), F32))
    for pair in range(4):
        high, low = halves(jnp.concatenate(blocks[2 * pair : 2 * pair + 2], axis=1))
        weights[:, pair * 2 * DOF : (pair + 1) * 2 * DOF] = jnp.concatenate(
            [high, high, low, low], axis=0
        )

    def fill_table(first, number, hot, faces):
        flags, scale = table_of(hot, faces)
        table[rows_of(first, number), 0 : 6 * DOF] = flags
        table[rows_of(first, number), 6 * DOF : 8 * DOF] = scale

    fill_table(off - 1, layers, perm, tables_out[...])
    loads[7].wait()
    for step in range(COARSEN):
        one, two = permuted_pair(forcing_ref[step], forcing_ref[COARSEN + step])
        sources[0, step] = one
        sources[1, step] = two

    reach = 2 * HALO - 1 - layers
    spans = (
        (off - 1 - layers, 0, layers),
        (end - 1, 0, layers),
        (0, layers - reach, reach),
        (end - 1 + layers, 0, reach),
    )
    for slot, (place, begin, number) in enumerate(spans):
        tables_copies[slot].wait_recv()
        faces = tables_in[slot]
        hot = one_hot(faces[7:8].astype(jnp.int32), begin * LAYER, number * LAYER)
        fill_table(place, number, hot, faces)

    guess_copy.wait_recv()

    @pl.when(tme > 0)
    def _():
        one, _ = permuted_pair(guess_in[...], guess_in[...])
        ext_a[rows_of(off, layers), :] = one
        send_fine(0, 0, ext_a)

    def product(stage, zspan, xyspan):
        low, high = zspan
        rows = split[stage, low * LAYER : high * LAYER, :]
        prod[stage, low * LAYER : high * LAYER, 4 * DOF :] = jnp.dot(
            jnp.concatenate([rows, rows], axis=1),
            weights[:, 4 * DOF :],
            preferred_element_type=F32,
        )
        low, high = xyspan
        rows = split[stage, low * LAYER : high * LAYER, :]
        prod[stage, low * LAYER : high * LAYER, : 4 * DOF] = jnp.dot(
            jnp.concatenate([rows, rows], axis=1),
            weights[:, : 4 * DOF],
            preferred_element_type=F32,
        )

    def combined(stage, layer):
        base = layer * LAYER
        here = slice(base, base + LAYER)
        left = left_lanes(LAYER)
        left3 = left.reshape(LAYER // GX, GX, 2 * DOF)
        px = prod[stage, here, 0 : 2 * DOF].reshape(LAYER // GX, GX, 2 * DOF)
        xs = jnp.where(left3, pltpu.roll(px, GX - 1, 1), pltpu.roll(px, 1, 1))
        py = prod[stage, here, 2 * DOF : 4 * DOF].reshape(LAYER // GX, GX, 2 * DOF)
        ys = jnp.where(
            left3,
            jnp.concatenate([py[1:], py[:1]], axis=0),
            jnp.concatenate([py[-1:], py[:-1]], axis=0),
        )
        zs = jnp.where(
            left,
            prod[stage, base + LAYER : base + 2 * LAYER, 4 * DOF : 6 * DOF],
            prod[stage, base - LAYER : base, 4 * DOF : 6 * DOF],
        )
        own_term = prod[stage, here, 6 * DOF : 8 * DOF]
        tab = slice(base - LAYER, base)
        total = (
            table[tab, 0 : 2 * DOF] * xs.reshape(LAYER, 2 * DOF)
            + table[tab, 2 * DOF : 4 * DOF] * ys.reshape(LAYER, 2 * DOF)
        ) + (
            table[tab, 4 * DOF : 6 * DOF] * zs
            + table[tab, 6 * DOF : 8 * DOF] * own_term
        )
        return total + swapped(total)

    def store_split(stage, layer, value):
        low = value - value.astype(BF16).astype(F32)
        split[stage, layer * LAYER : (layer + 1) * LAYER, :] = jnp.where(
            left_lanes(LAYER), value, low
        ).astype(BF16)

    def advance(x, size, stage, layer, finish):
        here = slice(layer * LAYER, (layer + 1) * LAYER)
        value = x[here, :] + size / (4 - stage) * combined(stage, layer)
        if stage < 3:
            store_split(stage + 1, layer, value)
        else:
            finish(layer, value)

    def inner_step(x, size, finish):
        low, high = off - HALO, end + HALO
        for layer in range(low, high):
            store_split(0, layer, x[layer * LAYER : (layer + 1) * LAYER, :])
        for stage in range(4):
            product(stage, (low + stage, high - stage), (low + stage + 1, high - stage - 1))
            for layer in range(low + stage + 1, high - stage - 1):
                advance(x, size, stage, layer, finish)

    def outer_step(x, size, finish):
        last = end + 2 * HALO
        for layer in (*range(HALO), *range(last - HALO, last)):
            store_split(0, layer, x[layer * LAYER : (layer + 1) * LAYER, :])
        for stage in range(4):
            sides = (
                ((stage, stage + HALO), (stage + 1, stage + 1 + HALO)),
                (
                    (last - stage - HALO, last - stage),
                    (last - stage - 1 - HALO, last - stage - 1),
                ),
            )
            for zspan, xyspan in sides:
                product(stage, zspan, xyspan)
            for _, xyspan in sides:
                for layer in range(*xyspan):
                    advance(x, size, stage, layer, finish)

    def residual_copies(index):
        point = count * tme + index
        result = []
        for step in range(times - 1, 0, -1):
            result.append((
                step,
                pltpu.make_async_remote_copy(
                    src_ref=res_out.at[index],
                    dst_ref=res_in.at[point],
                    send_sem=res_send.at[index, step],
                    recv_sem=res_recv.at[point],
                    device_id=(lax.rem(tme + step, times), sme),
                    device_id_type=MESH,
                ),
            ))
        return result

    def fine(step, carry):
        for point, ext in ((1, ext_b), (0, ext_a)):
            receive_fine(point, step, ext)

            def finish(layer, value):
                inside = rows_of(layer - off)
                ext[rows_of(layer), :] = value + sources[point, step, inside, :]

            inner_step(ext, 1.0, finish)

            @pl.when(step < COARSEN - 1)
            def _():
                send_fine(point, step + 1, ext)

            @pl.when(step == COARSEN - 1)
            def _():
                index = count * tme + point
                errors[index] = ext[rows_of(off, layers), :] - guess_grid[point]
                pack(res_out.at[point], errors.at[index], 0, layers // 2)
                for distance, copy in residual_copies(point):

                    @pl.when(tme + distance < times)
                    def _():
                        copy.start()

        return carry

    lax.fori_loop(0, COARSEN, fine, 0)

    final = count * tme + count - 1

    def take_residual(point):
        @pl.when(point < count * tme)
        def _():
            pltpu.make_async_remote_copy(
                src_ref=res_out.at[0],
                dst_ref=res_in.at[point],
                send_sem=res_send.at[0, 0],
                recv_sem=res_recv.at[point],
                device_id=(lax.rem(tme + 1, times), sme),
                device_id_type=MESH,
            ).wait_recv()
            unpack(res_in.at[point], errors.at[point], 0, layers // 2)

    def edge_copies(point):
        return [
            pltpu.make_async_remote_copy(
                src_ref=edge_out.at[point, side],
                dst_ref=edge_in.at[point, side],
                send_sem=edge_send.at[point, side],
                recv_sem=edge_recv.at[point, side],
                device_id=(tme, around[side]),
                device_id_type=MESH,
            )
            for side in range(2)
        ]

    def send_edges(point):
        pack(edge_out.at[point, 0], errors.at[point], layers - HALO, half)
        pack(edge_out.at[point, 1], errors.at[point], 0, half)
        for copy in edge_copies(point):
            copy.start()

    def piece_copies(point):
        return [
            pltpu.make_async_remote_copy(
                src_ref=piece_out.at[point, (0, 1, 1, 0)[slot]],
                dst_ref=piece_in.at[point, slot],
                send_sem=piece_send.at[point, slot],
                recv_sem=piece_recv.at[point, slot],
                device_id=(tme, around[slot]),
                device_id_type=MESH,
            )
            for slot in range(4)
        ]

    def send_pieces(point):
        pack(piece_out.at[point, 0], ext_a, off, 1)
        pack(piece_out.at[point, 1], ext_a, end - 2, 1)
        for copy in piece_copies(point):
            copy.start()

    def receive_pieces(point):
        places = (off - layers, end + layers - 2, 0, end + layers)
        for slot, copy in enumerate(piece_copies(point)):
            copy.wait_recv()
            unpack(piece_in.at[point, slot], ext_a, places[slot], 1)

    def receive_edges(point, place):
        for side, copy in enumerate(edge_copies(point)):
            copy.wait_recv()
            place(side, edge_in.at[point, side])

    take_residual(0)
    send_edges(0)
    ext_a[rows_of(off, layers), :] = errors[0]

    @pl.when(final > 1)
    def _():
        send_pieces(0)

    receive_edges(0, lambda side, ref: unpack(ref, ext_a, off - HALO if side == 0 else end, half))

    def coarse(point, carry):
        take_residual(point)

        @pl.when(point < final)
        def _():
            send_edges(point)

        def finish(layer, value):
            inside = rows_of(layer - off)
            value = value + errors[point, inside, :]
            ext_a[rows_of(layer), :] = value
            errors[point, inside, :] = value

        inner_step(ext_a, float(COARSEN), finish)

        @pl.when(point < final - 1)
        def _():
            send_pieces(point)

        @pl.when(point < final)
        def _():
            receive_pieces(point - 1)
            receive_edges(
                point, lambda side, ref: unpack(ref, ext_b, off - HALO if side == 0 else end, half)
            )

            def finish_outer(layer, value):
                ext_a[rows_of(layer), :] = value + ext_b[rows_of(layer), :]

            outer_step(ext_a, float(COARSEN), finish_outer)

        return carry

    lax.fori_loop(1, final + 1, coarse, 0)

    packed = jnp.where(left_lanes(own), errors[final - 1], errors[final])
    parts = [
        lax.dot_general(part, perm_ref[...], (((0,), (0,)), ((), ())), preferred_element_type=F32)
        for part in thirds(packed)
    ]
    result = (parts[0] + parts[1]) + parts[2]
    out_ref[0] = result[:DOF]
    out_ref[1] = result[DOF:]

    guess_copy.wait_send()
    for copy in tables_copies:
        copy.wait_send()

    def fine_done(step, carry):
        for point in range(2):
            for copy in fine_copies(point, step):
                copy.wait_send()
        return carry

    lax.fori_loop(0, COARSEN, fine_done, 0)
    for index in range(2):
        for distance, copy in residual_copies(index):

            @pl.when(tme + distance < times)
            def _():
                copy.wait_send()

    def sweep_done(point, carry):
        for copy in edge_copies(point):
            copy.wait_send()

        @pl.when(point < final - 1)
        def _():
            for copy in piece_copies(point):
                copy.wait_send()

        return carry

    lax.fori_loop(0, final, sweep_done, 0)


def body(init_state, guess, forcing, volume_block, face_blocks, elem_scales, element_ids, neighbours, walls):
    own = element_ids.shape[0]
    layers = own // LAYER
    count = guess.shape[0]
    times = lax.axis_size("tm")
    points = times * count
    ext = (layers + 4 * HALO) * LAYER
    wide = 2 * DOF
    vmem = pltpu.VMEM
    dma = pltpu.SemaphoreType.DMA
    errors = pl.pallas_call(
        functools.partial(kernel, layers, count),
        out_shape=jax.ShapeDtypeStruct(guess.shape, F32),
        in_specs=[pl.BlockSpec(memory_space=pl.ANY)] * 8,
        out_specs=pl.BlockSpec(memory_space=pltpu.VMEM),
        scratch_shapes=[
            vmem(init_state.shape, F32),
            vmem(guess.shape, F32),
            vmem(forcing.shape, F32),
            vmem(volume_block.shape, F32),
            vmem(face_blocks.shape, F32),
            vmem((1, own), F32),
            vmem((1, own), jnp.int32),
            vmem(walls.shape, jnp.int32),
            vmem((4 * DOF, 8 * DOF), BF16),
            vmem((ext - 2 * LAYER, 8 * DOF), F32),
            vmem((own, own), BF16),
            vmem((2, COARSEN, own, wide), F32),
            vmem((2, own, wide), F32),
            vmem((ext, wide), F32),
            vmem((ext, wide), F32),
            vmem((4, ext, wide), BF16),
            vmem((4, ext, 8 * DOF), F32),
            vmem((points, own, wide), F32),
            vmem((8, own), F32),
            vmem((4, 8, own), F32),
            vmem((DOF, own), F32),
            vmem((2, COARSEN, 2, HALO // 2 * LAYER, wide), F32),
            vmem((2, COARSEN, 2, HALO // 2 * LAYER, wide), F32),
            vmem((points, 2, LAYER, wide), F32),
            vmem((points, 4, LAYER, wide), F32),
            vmem((points, 2, HALO // 2 * LAYER, wide), F32),
            vmem((points, 2, HALO // 2 * LAYER, wide), F32),
            vmem((2, own // 2, wide), F32),
            vmem((points, own // 2, wide), F32),
            dma((8,)),
            dma((4,)),
            dma((4,)),
            dma,
            dma,
            dma((2, COARSEN, 2)),
            dma((2, COARSEN, 2)),
            dma((points, 4)),
            dma((points, 4)),
            dma((points, 2)),
            dma((points, 2)),
            dma((2, times)),
            dma((points,)),
        ],
        compiler_params=pltpu.CompilerParams(
            collective_id=0, has_side_effects=True, vmem_limit_bytes=56 * 1024 * 1024
        ),
    )(
        init_state,
        guess,
        forcing,
        volume_block,
        face_blocks,
        elem_scales.reshape(1, own),
        element_ids.reshape(1, own),
        walls,
    )
    return guess + errors


def solution(mesh):
    return jax.shard_map(
        body,
        mesh=mesh,
        in_specs=(
            P(None, "space"),
            P("tm", None, "space"),
            P("tm", None, "space"),
            P(),
            P(),
            P("space"),
            P("space"),
            P(None, "space"),
            P(None, "space"),
        ),
        out_specs=P("tm", None, "space"),
        check_vma=False,
    )
```

time: 96.9 us -> 85.8 us (0.89)
  the two profiles are of different devices: /device:TPU:4 before, /device:TPU:6 now
where the time goes in v2:
time: 85.8 us; the launch traced here: 85.7 us
  Pallas kernels  82.2 us (96%)
  local copies, waits for them, and re-layouts  1.83 us (2%)
  other arithmetic  1.63 us (2%)
    pallas_call x1, Pallas kernels, body(): pl.pallas_call(functools.partial(kernel, layers, count), out_shape=jax.Sh...  82.2 us

profile of v2, /device:TPU:6, one launch (start us, length us, event | category | flops | bytes accessed | tf_op | source)
XLA Modules:
  0.0 85.7 jit_solution(11825764709065900624)
XLA Ops:
  0.0 0.0 copy-start.1
  0.0 1.3 %reshape.6.scales_hbm = f32[1,384]{1,0:T(1,128)} reshape(f32[384]{0:T(512)} %param.14) | data formatting | bytes 3072 | tf_op jit(solution)/shard_map/reshape | solution.py:645
  1.3 0.0 copy-done.1
  1.3 0.6 reshape.7.ids_hbm
  1.8 0.0 copy-start
  1.8 82.2 %shard_map.82 = f32[2,64,384]{2,1,0:T(8,128)} custom-call(f32[64,384]{1,0:T(8,128)} %init_hbm.1, f32[2,64,384]{2,1,0:T(8,128)} %guess_hbm.1, f32[8,64,384]{2,1,0:T(8,128)} %forcing_hbm.1, f32[64,64]{1,0:T(8,128)} %volume_hbm.1, f32[3,64,64]{2,1,0:T(8,128)} %faces_hbm.1, f32[1,384]{1,0:T(1,128)} %reshape.6.scales_hbm, s32[1,384]{1,0:T(1,128)} %reshape.7.ids_hbm, ...), custom_call_target="tpu_custom_call" | custom-call | tf_op jit(solution)/shard_map/pallas_call | solution.py:587
  84.0 0.0 copy-done
  84.0 1.6 %add.3 = f32[2,64,384]{2,1,0:T(8,128)} add(f32[2,64,384]{2,1,0:T(8,128)S(1)} %copy-done, f32[2,64,384]{2,1,0:T(8,128)} %shard_map.82) | non-fusion elementwise | flops 49152 | bytes 589824 | tf_op jit(solution)/shard_map/add | solution.py:649
Async XLA Ops:
  0.0 1.3 %copy-start.1 = (s32[384]{0:T(512)S(1)}, s32[384]{0:T(512)}, u32[]{:S(2)}) copy-start(s32[384]{0:T(512)} %param.15) | copy-start | bytes 4612
  1.8 82.2 %copy-start = (f32[2,64,384]{2,1,0:T(8,128)S(1)}, f32[2,64,384]{2,1,0:T(8,128)}, u32[]{:S(2)}) copy-start(f32[2,64,384]{2,1,0:T(8,128)} %guess_hbm.1) | copy-start | bytes 589828

commit v3 on v2

--- a/solution.py
+++ b/solution.py
@@ -89,16 +89,20 @@
     perm_ref,
     sources,
     guess_grid,
-    ext_a,
-    ext_b,
+    exts,
+    spare,
     split,
     prod,
     errors,
     tables_out,
     tables_in,
     guess_in,
-    fine_out,
-    fine_in,
+    block_out,
+    block_in,
+    strip_out,
+    strip_in,
+    force_out,
+    force_in,
     piece_out,
     piece_in,
     edge_out,
@@ -110,8 +114,12 @@
     tables_recv,
     guess_send,
     guess_recv,
-    fine_send,
-    fine_recv,
+    block_send,
+    block_recv,
+    strip_send,
+    strip_recv,
+    force_send,
+    force_recv,
     piece_send,
     piece_recv,
     edge_send,
@@ -124,6 +132,7 @@
     tme = lax.axis_index("tm")
     sme = lax.axis_index("space")
     own = layers * LAYER
+    ext_a = exts.at[0]
     off = 2 * HALO
     end = off + layers
     around = [lax.rem(sme + spaces + step, spaces) for step in (1, -1, 2, -2)]
@@ -155,9 +164,9 @@
 
     for copy in loads[:3]:
         copy.wait()
-    local = ids_ref[...] - sme * own
+    local = ids_ref[...].reshape(1, own) - sme * own
     tables_out[0:6, :] = (1 - walls_ref[...]).astype(F32)
-    tables_out[6:7, :] = scales_ref[...]
+    tables_out[6:7, :] = scales_ref[...].reshape(1, own)
     tables_out[7:8, :] = local.astype(F32)
     perm = one_hot(local, 0, own)
     perm_ref[...] = perm
@@ -169,7 +178,7 @@
     one, two = permuted_pair(guess_ref[0], guess_ref[1])
     guess_grid[0] = one
     guess_grid[1] = two
-    ext_b[rows_of(off, layers), :] = one
+    exts[1, rows_of(off, layers), :] = one
 
     def pack(target, source, first, number):
         for layer in range(number):
@@ -187,29 +196,92 @@
 
     half = HALO // 2
 
-    def fine_copies(point, step):
-        return [
-            pltpu.make_async_remote_copy(
-                src_ref=fine_out.at[point, step, side],
-                dst_ref=fine_in.at[point, step, side],
-                send_sem=fine_send.at[point, step, side],
-                recv_sem=fine_recv.at[point, step, side],
-                device_id=(tme, around[side]),
-                device_id_type=MESH,
+    def remote(source, target, send, recv, slot):
+        return pltpu.make_async_remote_copy(
+            src_ref=source,
+            dst_ref=target,
+            send_sem=send,
+            recv_sem=recv,
+            device_id=(tme, around[slot]),
+            device_id_type=MESH,
+        )
+
+    def state_copies(point, turn):
+        copies = [
+            remote(
+                block_out.at[point, turn],
+                block_in.at[point, turn, side],
+                block_send.at[point, turn, side],
+                block_recv.at[point, turn, side],
+                side,
             )
             for side in range(2)
         ]
-
-    def send_fine(point, step, ext):
-        pack(fine_out.at[point, step, 0], ext, end - HALO, half)
-        pack(fine_out.at[point, step, 1], ext, off, half)
-        for copy in fine_copies(point, step):
+        return copies + [
+            remote(
+                strip_out.at[point, turn, side],
+                strip_in.at[point, turn, side],
+                strip_send.at[point, turn, side],
+                strip_recv.at[point, turn, side],
+                2 + side,
+            )
+            for side in range(2)
+        ]
+
+    def send_state(point, turn):
+        ext = exts.at[point]
+        pack(block_out.at[point, turn], ext, off, layers // 2)
+        pack(strip_out.at[point, turn, 0], ext, end - 2, 1)
+        pack(strip_out.at[point, turn, 1], ext, off, 1)
+        for copy in state_copies(point, turn):
             copy.start()
 
-    def receive_fine(point, step, ext):
-        for side, copy in enumerate(fine_copies(point, step)):
+    def receive_state(point, turn):
+        ext = exts.at[point]
+        copies = state_copies(point, turn)
+        for copy in copies:
             copy.wait_recv()
-            unpack(fine_in.at[point, step, side], ext, off - HALO if side == 0 else end, half)
+        unpack(block_in.at[point, turn, 0], ext, off - layers, layers // 2)
+        unpack(block_in.at[point, turn, 1], ext, end, layers // 2)
+        unpack(strip_in.at[point, turn, 0], ext, off - layers - 2, 1)
+        unpack(strip_in.at[point, turn, 1], ext, end + layers, 1)
+
+    def force_copies(point, turn):
+        return [
+            remote(
+                force_out.at[point, turn, side],
+                force_in.at[point, turn, side],
+                force_send.at[point, turn, side],
+                force_recv.at[point, turn, side],
+                side,
+            )
+            for side in range(2)
+        ]
+
+    def send_force(point, turn):
+        source = sources.at[point, 2 * turn]
+        pack(force_out.at[point, turn, 0], source, layers, half)
+        pack(force_out.at[point, turn, 1], source, HALO, half)
+        for copy in force_copies(point, turn):
+            copy.start()
+
+    def receive_force(point, turn):
+        for side, copy in enumerate(force_copies(point, turn)):
+            copy.wait_recv()
+            unpack(
+                force_in.at[point, turn, side],
+                sources.at[point, 2 * turn],
+                0 if side == 0 else HALO + layers,
+                half,
+            )
+
+    for copy in loads[4:7]:
+        copy.wait()
+
+    @pl.when(tme == 0)
+    def _():
+        one, _ = permuted_pair(init_ref[...], init_ref[...])
+        exts[0, rows_of(off, layers), :] = one
 
     pl.semaphore_wait(barrier, 4 + times - 1)
 
@@ -235,16 +307,20 @@
     ]
     for copy in tables_copies:
         copy.start()
-    send_fine(1, 0, ext_b)
-
-    for copy in loads[4:7]:
-        copy.wait()
 
     @pl.when(tme == 0)
     def _():
-        one, _ = permuted_pair(init_ref[...], init_ref[...])
-        ext_a[rows_of(off, layers), :] = one
-        send_fine(0, 0, ext_a)
+        send_state(0, 0)
+
+    send_state(1, 0)
+    loads[7].wait()
+    for step in (0, 2, 1, 3):
+        one, two = permuted_pair(forcing_ref[step], forcing_ref[COARSEN + step])
+        sources[0, step, rows_of(HALO, layers), :] = one
+        sources[1, step, rows_of(HALO, layers), :] = two
+        if step == 0:
+            send_force(1, 0)
+            send_force(0, 0)
 
     blocks = []
     for m in range(3):
@@ -265,12 +341,6 @@
         table[rows_of(first, number), 6 * DOF : 8 * DOF] = scale
 
     fill_table(off - 1, layers, perm, tables_out[...])
-    loads[7].wait()
-    for step in range(COARSEN):
-        one, two = permuted_pair(forcing_ref[step], forcing_ref[COARSEN + step])
-        sources[0, step] = one
-        sources[1, step] = two
-
     reach = 2 * HALO - 1 - layers
     spans = (
         (off - 1 - layers, 0, layers),
@@ -289,8 +359,11 @@
     @pl.when(tme > 0)
     def _():
         one, _ = permuted_pair(guess_in[...], guess_in[...])
-        ext_a[rows_of(off, layers), :] = one
-        send_fine(0, 0, ext_a)
+        exts[0, rows_of(off, layers), :] = one
+        send_state(0, 0)
+
+    send_force(1, 1)
+    send_force(0, 1)
 
     def product(stage, zspan, xyspan):
         low, high = zspan
@@ -351,14 +424,16 @@
         else:
             finish(layer, value)
 
-    def inner_step(x, size, finish):
-        low, high = off - HALO, end + HALO
+    def whole_step(x, size, low, high, finish):
         for layer in range(low, high):
             store_split(0, layer, x[layer * LAYER : (layer + 1) * LAYER, :])
         for stage in range(4):
             product(stage, (low + stage, high - stage), (low + stage + 1, high - stage - 1))
             for layer in range(low + stage + 1, high - stage - 1):
                 advance(x, size, stage, layer, finish)
+
+    def inner_step(x, size, finish):
+        whole_step(x, size, off - HALO, end + HALO, finish)
 
     def outer_step(x, size, finish):
         last = end + 2 * HALO
@@ -395,34 +470,41 @@
             ))
         return result
 
-    def fine(step, carry):
-        for point, ext in ((1, ext_b), (0, ext_a)):
-            receive_fine(point, step, ext)
-
-            def finish(layer, value):
-                inside = rows_of(layer - off)
-                ext[rows_of(layer), :] = value + sources[point, step, inside, :]
-
-            inner_step(ext, 1.0, finish)
-
-            @pl.when(step < COARSEN - 1)
-            def _():
-                send_fine(point, step + 1, ext)
-
-            @pl.when(step == COARSEN - 1)
-            def _():
-                index = count * tme + point
-                errors[index] = ext[rows_of(off, layers), :] - guess_grid[point]
-                pack(res_out.at[point], errors.at[index], 0, layers // 2)
-                for distance, copy in residual_copies(point):
-
-                    @pl.when(tme + distance < times)
-                    def _():
-                        copy.start()
+    def fine(index, carry):
+        turn = index // 2
+        point = lax.rem(index + jnp.minimum(tme, 1), 2)
+        ext = exts.at[point]
+        receive_state(point, turn)
+        receive_force(point, turn)
+
+        def finish(step):
+            def store(layer, value):
+                there = rows_of(layer - off + HALO)
+                ext[rows_of(layer), :] = value + sources[point, 2 * turn + step, there, :]
+
+            return store
+
+        whole_step(ext, 1.0, off - 2 * HALO, end + 2 * HALO, finish(0))
+        inner_step(ext, 1.0, finish(1))
+
+        @pl.when(turn == 0)
+        def _():
+            send_state(point, 1)
+
+        @pl.when(turn == 1)
+        def _():
+            place = count * tme + point
+            errors[place] = ext[rows_of(off, layers), :] - guess_grid[point]
+            pack(res_out.at[point], errors.at[place], 0, layers // 2)
+            for distance, copy in residual_copies(point):
+
+                @pl.when(tme + distance < times)
+                def _():
+                    copy.start()
 
         return carry
 
-    lax.fori_loop(0, COARSEN, fine, 0)
+    lax.fori_loop(0, 4, fine, 0)
 
     final = count * tme + count - 1
 
@@ -488,23 +570,28 @@
             copy.wait_recv()
             place(side, edge_in.at[point, side])
 
-    take_residual(0)
-    send_edges(0)
+    def pass_residual(point):
+        @pl.when(point <= final)
+        def _():
+            take_residual(point)
+
+        @pl.when(point < final)
+        def _():
+            send_edges(point)
+
+    pass_residual(0)
     ext_a[rows_of(off, layers), :] = errors[0]
 
     @pl.when(final > 1)
     def _():
         send_pieces(0)
 
+    pass_residual(1)
+    pass_residual(2)
+
     receive_edges(0, lambda side, ref: unpack(ref, ext_a, off - HALO if side == 0 else end, half))
 
     def coarse(point, carry):
-        take_residual(point)
-
-        @pl.when(point < final)
-        def _():
-            send_edges(point)
-
         def finish(layer, value):
             inside = rows_of(layer - off)
             value = value + errors[point, inside, :]
@@ -517,15 +604,17 @@
         def _():
             send_pieces(point)
 
+        pass_residual(point + 2)
+
         @pl.when(point < final)
         def _():
             receive_pieces(point - 1)
             receive_edges(
-                point, lambda side, ref: unpack(ref, ext_b, off - HALO if side == 0 else end, half)
+                point, lambda side, ref: unpack(ref, spare, off - HALO if side == 0 else end, half)
             )
 
             def finish_outer(layer, value):
-                ext_a[rows_of(layer), :] = value + ext_b[rows_of(layer), :]
+                ext_a[rows_of(layer), :] = value + spare[rows_of(layer), :]
 
             outer_step(ext_a, float(COARSEN), finish_outer)
 
@@ -546,13 +635,10 @@
     for copy in tables_copies:
         copy.wait_send()
 
-    def fine_done(step, carry):
-        for point in range(2):
-            for copy in fine_copies(point, step):
+    for point in range(2):
+        for turn in range(2):
+            for copy in state_copies(point, turn) + force_copies(point, turn):
                 copy.wait_send()
-        return carry
-
-    lax.fori_loop(0, COARSEN, fine_done, 0)
     for index in range(2):
         for distance, copy in residual_copies(index):
 
@@ -595,15 +681,15 @@
             vmem(forcing.shape, F32),
             vmem(volume_block.shape, F32),
             vmem(face_blocks.shape, F32),
-            vmem((1, own), F32),
-            vmem((1, own), jnp.int32),
+            vmem((own,), F32),
+            vmem((own,), jnp.int32),
             vmem(walls.shape, jnp.int32),
             vmem((4 * DOF, 8 * DOF), BF16),
             vmem((ext - 2 * LAYER, 8 * DOF), F32),
             vmem((own, own), BF16),
-            vmem((2, COARSEN, own, wide), F32),
+            vmem((2, COARSEN, own + 2 * HALO * LAYER, wide), F32),
             vmem((2, own, wide), F32),
-            vmem((ext, wide), F32),
+            vmem((2, ext, wide), F32),
             vmem((ext, wide), F32),
             vmem((4, ext, wide), BF16),
             vmem((4, ext, 8 * DOF), F32),
@@ -611,8 +697,12 @@
             vmem((8, own), F32),
             vmem((4, 8, own), F32),
             vmem((DOF, own), F32),
-            vmem((2, COARSEN, 2, HALO // 2 * LAYER, wide), F32),
-            vmem((2, COARSEN, 2, HALO // 2 * LAYER, wide), F32),
+            vmem((2, 2, own // 2, wide), F32),
+            vmem((2, 2, 2, own // 2, wide), F32),
+            vmem((2, 2, 2, LAYER, wide), F32),
+            vmem((2, 2, 2, LAYER, wide), F32),
+            vmem((2, 2, 2, HALO // 2 * LAYER, wide), F32),
+            vmem((2, 2, 2, HALO // 2 * LAYER, wide), F32),
             vmem((points, 2, LAYER, wide), F32),
             vmem((points, 4, LAYER, wide), F32),
             vmem((points, 2, HALO // 2 * LAYER, wide), F32),
@@ -624,8 +714,12 @@
             dma((4,)),
             dma,
             dma,
-            dma((2, COARSEN, 2)),
-            dma((2, COARSEN, 2)),
+            dma((2, 2, 2)),
+            dma((2, 2, 2)),
+            dma((2, 2, 2)),
+            dma((2, 2, 2)),
+            dma((2, 2, 2)),
+            dma((2, 2, 2)),
             dma((points, 4)),
             dma((points, 4)),
             dma((points, 2)),
@@ -642,8 +736,8 @@
         forcing,
         volume_block,
         face_blocks,
-        elem_scales.reshape(1, own),
-        element_ids.reshape(1, own),
+        elem_scales,
+        element_ids,
         walls,
     )
     return guess + errors

time: 85.8 us -> 67.3 us (0.78)
  Pallas kernels: 82.2 us -> 65.5 us
  local copies, waits for them, and re-layouts: 1.83 us -> 0.01 us
    pallas_call x1, Pallas kernels: 82.2 us -> 65.5 us  [body(): pl.pallas_call(functools.partial(kernel, layers, count), out_shape=jax.Sh...]
    reshape x2 -> x0, local copies, waits for them, and re-layouts: 1.82 us -> none  [the longest x1 1.26 us: body(): elem_scales.reshape(1, own)]
where the time goes in v3:
time: 67.3 us; the launch traced here: 67.2 us
  Pallas kernels  65.5 us (97%)
  other arithmetic  1.63 us (2%)
    pallas_call x1, Pallas kernels, body(): pl.pallas_call(functools.partial(kernel, layers, count), out_shape=jax.Sh...  65.5 us
    add x1, other arithmetic, body(): return guess + errors  1.63 us

profile of v3, /device:TPU:6, one launch (start us, length us, event | category | flops | bytes accessed | tf_op | source)
XLA Modules:
  0.0 67.2 jit_solution(4197208973537794734)
XLA Ops:
  0.0 0.0 copy-start
  0.0 65.5 %shard_map.82 = f32[2,64,384]{2,1,0:T(8,128)} custom-call(f32[64,384]{1,0:T(8,128)} %init_hbm.1, f32[2,64,384]{2,1,0:T(8,128)} %guess_hbm.1, f32[8,64,384]{2,1,0:T(8,128)} %forcing_hbm.1, f32[64,64]{1,0:T(8,128)} %volume_hbm.1, f32[3,64,64]{2,1,0:T(8,128)} %faces_hbm.1, f32[384]{0:T(512)} %scales_hbm.1, s32[384]{0:T(512)} %ids_hbm.1, s32[6,384]{1,0:T(8,128)} %walls_hbm.1), custom_call_target="tpu_custom_call" | custom-call | tf_op jit(solution)/shard_map/pallas_call | solution.py:673
  65.5 0.0 copy-done
  65.6 1.6 %add.3 = f32[2,64,384]{2,1,0:T(8,128)} add(f32[2,64,384]{2,1,0:T(8,128)S(1)} %copy-done, f32[2,64,384]{2,1,0:T(8,128)} %shard_map.82) | non-fusion elementwise | flops 49152 | bytes 589824 | tf_op jit(solution)/shard_map/add | solution.py:743
Async XLA Ops:
  0.0 65.5 %copy-start = (f32[2,64,384]{2,1,0:T(8,128)S(1)}, f32[2,64,384]{2,1,0:T(8,128)}, u32[]{:S(2)}) copy-start(f32[2,64,384]{2,1,0:T(8,128)} %guess_hbm.1) | copy-start | bytes 589828

commit v4 on v3

--- a/solution.py
+++ b/solution.py
@@ -136,6 +136,38 @@
     off = 2 * HALO
     end = off + layers
     around = [lax.rem(sme + spaces + step, spaces) for step in (1, -1, 2, -2)]
+    heard = [sme >= 1, sme <= spaces - 2, sme >= 2, sme <= spaces - 3]
+    sent = [heard[1], heard[0], heard[3], heard[2]]
+
+    def start(copies):
+        for slot, copy in copies:
+            pl.when(sent[slot])(copy.start)
+
+    def arrive(copies):
+        for slot, copy in copies:
+            pl.when(heard[slot])(copy.wait_recv)
+
+    def finish_sends(copies):
+        for slot, copy in copies:
+            pl.when(sent[slot])(copy.wait_send)
+
+    for slot in range(4):
+
+        @pl.when(jnp.logical_not(heard[slot]))
+        def _():
+            tables_in[slot] = jnp.zeros(tables_in.shape[1:], F32)
+            for point in range(times * count):
+                piece_in[point, slot] = jnp.zeros(piece_in.shape[2:], F32)
+                if slot < 2:
+                    edge_in[point, slot] = jnp.zeros(edge_in.shape[2:], F32)
+            for point in range(2):
+                for turn in range(2):
+                    if slot < 2:
+                        block_in[point, turn, slot] = jnp.zeros(block_in.shape[3:], F32)
+                        force_in[point, turn, slot] = jnp.zeros(force_in.shape[3:], F32)
+                    else:
+                        strip_in[point, turn, slot - 2] = jnp.zeros(strip_in.shape[3:], F32)
+
 
     pairs = (
         (ids_hbm, ids_ref),
@@ -152,8 +184,12 @@
         copy.start()
 
     barrier = pltpu.get_barrier_semaphore()
-    for device in around:
-        pl.semaphore_signal(barrier, inc=1, device_id=(tme, device), device_id_type=MESH)
+    for slot in range(4):
+
+        @pl.when(sent[slot])
+        def _():
+            pl.semaphore_signal(barrier, inc=1, device_id=(tme, around[slot]), device_id_type=MESH)
+
     for step in range(1, times):
         pl.semaphore_signal(
             barrier, inc=1, device_id=(lax.rem(tme + step, times), sme), device_id_type=MESH
@@ -208,23 +244,23 @@
 
     def state_copies(point, turn):
         copies = [
-            remote(
+            (side, remote(
                 block_out.at[point, turn],
                 block_in.at[point, turn, side],
                 block_send.at[point, turn, side],
                 block_recv.at[point, turn, side],
                 side,
-            )
+            ))
             for side in range(2)
         ]
         return copies + [
-            remote(
+            (2 + side, remote(
                 strip_out.at[point, turn, side],
                 strip_in.at[point, turn, side],
                 strip_send.at[point, turn, side],
                 strip_recv.at[point, turn, side],
                 2 + side,
-            )
+            ))
             for side in range(2)
         ]
 
@@ -233,14 +269,11 @@
         pack(block_out.at[point, turn], ext, off, layers // 2)
         pack(strip_out.at[point, turn, 0], ext, end - 2, 1)
         pack(strip_out.at[point, turn, 1], ext, off, 1)
-        for copy in state_copies(point, turn):
-            copy.start()
+        start(state_copies(point, turn))
 
     def receive_state(point, turn):
         ext = exts.at[point]
-        copies = state_copies(point, turn)
-        for copy in copies:
-            copy.wait_recv()
+        arrive(state_copies(point, turn))
         unpack(block_in.at[point, turn, 0], ext, off - layers, layers // 2)
         unpack(block_in.at[point, turn, 1], ext, end, layers // 2)
         unpack(strip_in.at[point, turn, 0], ext, off - layers - 2, 1)
@@ -248,32 +281,30 @@
 
     def force_copies(point, turn):
         return [
-            remote(
+            (side, remote(
                 force_out.at[point, turn, side],
                 force_in.at[point, turn, side],
                 force_send.at[point, turn, side],
                 force_recv.at[point, turn, side],
                 side,
-            )
+            ))
             for side in range(2)
         ]
 
     def send_force(point, turn):
         source = sources.at[point, 2 * turn]
-        pack(force_out.at[point, turn, 0], source, layers, half)
-        pack(force_out.at[point, turn, 1], source, HALO, half)
-        for copy in force_copies(point, turn):
-            copy.start()
-
-    def receive_force(point, turn):
-        for side, copy in enumerate(force_copies(point, turn)):
-            copy.wait_recv()
-            unpack(
-                force_in.at[point, turn, side],
-                sources.at[point, 2 * turn],
-                0 if side == 0 else HALO + layers,
-                half,
-            )
+        pack(force_out.at[point, turn, 0], source, layers - HALO, half)
+        pack(force_out.at[point, turn, 1], source, 0, half)
+        start(force_copies(point, turn))
+
+    def add_force(point, turn):
+        ext = exts.at[point]
+        arrive(force_copies(point, turn))
+        for side, first in enumerate((off - HALO, end)):
+            for layer in range(half):
+                one, two = doubled(force_in[point, turn, side, layer * LAYER : (layer + 1) * LAYER, :])
+                ext[rows_of(first + layer), :] = ext[rows_of(first + layer), :] + one
+                ext[rows_of(first + half + layer), :] = ext[rows_of(first + half + layer), :] + two
 
     for copy in loads[4:7]:
         copy.wait()
@@ -283,7 +314,7 @@
         one, _ = permuted_pair(init_ref[...], init_ref[...])
         exts[0, rows_of(off, layers), :] = one
 
-    pl.semaphore_wait(barrier, 4 + times - 1)
+    pl.semaphore_wait(barrier, times - 1 + sum(here.astype(jnp.int32) for here in heard))
 
     guess_copy = pltpu.make_async_remote_copy(
         src_ref=guess_ref.at[count - 1],
@@ -295,18 +326,10 @@
     )
     guess_copy.start()
     tables_copies = [
-        pltpu.make_async_remote_copy(
-            src_ref=tables_out,
-            dst_ref=tables_in.at[slot],
-            send_sem=tables_send.at[slot],
-            recv_sem=tables_recv.at[slot],
-            device_id=(tme, around[slot]),
-            device_id_type=MESH,
-        )
+        (slot, remote(tables_out, tables_in.at[slot], tables_send.at[slot], tables_recv.at[slot], slot))
         for slot in range(4)
     ]
-    for copy in tables_copies:
-        copy.start()
+    start(tables_copies)
 
     @pl.when(tme == 0)
     def _():
@@ -316,11 +339,11 @@
     loads[7].wait()
     for step in (0, 2, 1, 3):
         one, two = permuted_pair(forcing_ref[step], forcing_ref[COARSEN + step])
-        sources[0, step, rows_of(HALO, layers), :] = one
-        sources[1, step, rows_of(HALO, layers), :] = two
+        sources[0, step] = one
+        sources[1, step] = two
         if step == 0:
+            send_force(0, 0)
             send_force(1, 0)
-            send_force(0, 0)
 
     blocks = []
     for m in range(3):
@@ -349,7 +372,7 @@
         (end - 1 + layers, 0, reach),
     )
     for slot, (place, begin, number) in enumerate(spans):
-        tables_copies[slot].wait_recv()
+        arrive(tables_copies[slot : slot + 1])
         faces = tables_in[slot]
         hot = one_hot(faces[7:8].astype(jnp.int32), begin * LAYER, number * LAYER)
         fill_table(place, number, hot, faces)
@@ -365,93 +388,95 @@
     send_force(1, 1)
     send_force(0, 1)
 
-    def product(stage, zspan, xyspan):
-        low, high = zspan
-        rows = split[stage, low * LAYER : high * LAYER, :]
-        prod[stage, low * LAYER : high * LAYER, 4 * DOF :] = jnp.dot(
+    def split_of(value):
+        low = value - value.astype(BF16).astype(F32)
+        return jnp.where(left_lanes(LAYER), value, low).astype(BF16)
+
+    def products(blocks, part):
+        rows = jnp.concatenate(blocks, axis=0)
+        result = jnp.dot(
             jnp.concatenate([rows, rows], axis=1),
-            weights[:, 4 * DOF :],
+            weights[:, part * 4 * DOF : (part + 1) * 4 * DOF],
             preferred_element_type=F32,
         )
-        low, high = xyspan
-        rows = split[stage, low * LAYER : high * LAYER, :]
-        prod[stage, low * LAYER : high * LAYER, : 4 * DOF] = jnp.dot(
-            jnp.concatenate([rows, rows], axis=1),
-            weights[:, : 4 * DOF],
-            preferred_element_type=F32,
-        )
-
-    def combined(stage, layer):
-        base = layer * LAYER
-        here = slice(base, base + LAYER)
+        return [result[i * LAYER : (i + 1) * LAYER] for i in range(len(blocks))]
+
+    def combined(layer, flat, tall, below, above):
         left = left_lanes(LAYER)
         left3 = left.reshape(LAYER // GX, GX, 2 * DOF)
-        px = prod[stage, here, 0 : 2 * DOF].reshape(LAYER // GX, GX, 2 * DOF)
+        px = flat[:, : 2 * DOF].reshape(LAYER // GX, GX, 2 * DOF)
         xs = jnp.where(left3, pltpu.roll(px, GX - 1, 1), pltpu.roll(px, 1, 1))
-        py = prod[stage, here, 2 * DOF : 4 * DOF].reshape(LAYER // GX, GX, 2 * DOF)
+        py = flat[:, 2 * DOF :].reshape(LAYER // GX, GX, 2 * DOF)
         ys = jnp.where(
             left3,
             jnp.concatenate([py[1:], py[:1]], axis=0),
             jnp.concatenate([py[-1:], py[:-1]], axis=0),
         )
-        zs = jnp.where(
-            left,
-            prod[stage, base + LAYER : base + 2 * LAYER, 4 * DOF : 6 * DOF],
-            prod[stage, base - LAYER : base, 4 * DOF : 6 * DOF],
-        )
-        own_term = prod[stage, here, 6 * DOF : 8 * DOF]
-        tab = slice(base - LAYER, base)
+        zs = jnp.where(left, above[:, : 2 * DOF], below[:, : 2 * DOF])
+        tab = slice((layer - 1) * LAYER, layer * LAYER)
         total = (
             table[tab, 0 : 2 * DOF] * xs.reshape(LAYER, 2 * DOF)
             + table[tab, 2 * DOF : 4 * DOF] * ys.reshape(LAYER, 2 * DOF)
         ) + (
             table[tab, 4 * DOF : 6 * DOF] * zs
-            + table[tab, 6 * DOF : 8 * DOF] * own_term
+            + table[tab, 6 * DOF : 8 * DOF] * tall[:, 2 * DOF :]
         )
         return total + swapped(total)
 
-    def store_split(stage, layer, value):
-        low = value - value.astype(BF16).astype(F32)
-        split[stage, layer * LAYER : (layer + 1) * LAYER, :] = jnp.where(
-            left_lanes(LAYER), value, low
-        ).astype(BF16)
-
-    def advance(x, size, stage, layer, finish):
-        here = slice(layer * LAYER, (layer + 1) * LAYER)
-        value = x[here, :] + size / (4 - stage) * combined(stage, layer)
-        if stage < 3:
-            store_split(stage + 1, layer, value)
-        else:
-            finish(layer, value)
-
-    def whole_step(x, size, low, high, finish):
-        for layer in range(low, high):
-            store_split(0, layer, x[layer * LAYER : (layer + 1) * LAYER, :])
+    def here(layer):
+        return slice(layer * LAYER, (layer + 1) * LAYER)
+
+    def advance(x, size, stage, layers_, flat, tall, finish):
+        blocks = {}
+        for layer in layers_:
+            value = x[here(layer), :] + size / (4 - stage) * combined(
+                layer, flat[layer], tall[layer], tall[layer - 1], tall[layer + 1]
+            )
+            if stage < 3:
+                blocks[layer] = split_of(value)
+            else:
+                finish(layer, value)
+        return blocks
+
+    top = end + 2 * HALO
+
+    def whole_step(x, size, low, high, finish, keep=False):
+        blocks = {layer: split_of(x[here(layer), :]) for layer in range(low, high)}
         for stage in range(4):
-            product(stage, (low + stage, high - stage), (low + stage + 1, high - stage - 1))
-            for layer in range(low + stage + 1, high - stage - 1):
-                advance(x, size, stage, layer, finish)
-
-    def inner_step(x, size, finish):
-        whole_step(x, size, off - HALO, end + HALO, finish)
+            span = range(low + stage, high - stage)
+            inner = span[1:-1]
+            tall = dict(zip(span, products([blocks[layer] for layer in span], 1)))
+            flat = dict(zip(inner, products([blocks[layer] for layer in inner], 0)))
+            if keep:
+                split[stage, 0] = blocks[span[0]]
+                split[stage, 1] = blocks[span[-1]]
+                for place, layer in enumerate((span[0], span[1], span[-1], span[-2])):
+                    prod[stage, place] = tall[layer]
+            blocks = advance(x, size, stage, inner, flat, tall, finish)
+
+    def inner_step(x, size, finish, keep=True):
+        whole_step(x, size, off - HALO, end + HALO, finish, keep)
 
     def outer_step(x, size, finish):
-        last = end + 2 * HALO
-        for layer in (*range(HALO), *range(last - HALO, last)):
-            store_split(0, layer, x[layer * LAYER : (layer + 1) * LAYER, :])
+        lower = {layer: split_of(x[here(layer), :]) for layer in range(HALO)}
+        upper = {layer: split_of(x[here(layer), :]) for layer in range(top - HALO, top)}
         for stage in range(4):
-            sides = (
-                ((stage, stage + HALO), (stage + 1, stage + 1 + HALO)),
-                (
-                    (last - stage - HALO, last - stage),
-                    (last - stage - 1 - HALO, last - stage - 1),
-                ),
-            )
-            for zspan, xyspan in sides:
-                product(stage, zspan, xyspan)
-            for _, xyspan in sides:
-                for layer in range(*xyspan):
-                    advance(x, size, stage, layer, finish)
+            sides = []
+            for side, blocks in enumerate((lower, upper)):
+                first = stage if side == 0 else top - stage - HALO
+                span = range(first, first + HALO)
+                next_in = first + HALO if side == 0 else first - 1
+                second_in = next_in + 1 if side == 0 else next_in - 1
+                tall = dict(zip(span, products([blocks[layer] for layer in span], 1)))
+                tall[next_in] = prod[stage, 2 * side]
+                tall[second_in] = prod[stage, 2 * side + 1]
+                blocks[next_in] = split[stage, side]
+                inner = range(first + 1, first + 1 + HALO) if side == 0 else range(first - 1, first - 1 + HALO)
+                flat = dict(zip(inner, products([blocks[layer] for layer in inner], 0)))
+                sides.append((inner, flat, tall))
+            lower, upper = [
+                advance(x, size, stage, inner, flat, tall, finish) for inner, flat, tall in sides
+            ]
 
     def residual_copies(index):
         point = count * tme + index
@@ -475,17 +500,18 @@
         point = lax.rem(index + jnp.minimum(tme, 1), 2)
         ext = exts.at[point]
         receive_state(point, turn)
-        receive_force(point, turn)
 
         def finish(step):
             def store(layer, value):
-                there = rows_of(layer - off + HALO)
-                ext[rows_of(layer), :] = value + sources[point, 2 * turn + step, there, :]
+                if off <= layer < end:
+                    value = value + sources[point, 2 * turn + step, rows_of(layer - off), :]
+                ext[rows_of(layer), :] = value
 
             return store
 
         whole_step(ext, 1.0, off - 2 * HALO, end + 2 * HALO, finish(0))
-        inner_step(ext, 1.0, finish(1))
+        add_force(point, turn)
+        inner_step(ext, 1.0, finish(1), keep=False)
 
         @pl.when(turn == 0)
         def _():
@@ -523,51 +549,47 @@
 
     def edge_copies(point):
         return [
-            pltpu.make_async_remote_copy(
-                src_ref=edge_out.at[point, side],
-                dst_ref=edge_in.at[point, side],
-                send_sem=edge_send.at[point, side],
-                recv_sem=edge_recv.at[point, side],
-                device_id=(tme, around[side]),
-                device_id_type=MESH,
-            )
+            (side, remote(
+                edge_out.at[point, side],
+                edge_in.at[point, side],
+                edge_send.at[point, side],
+                edge_recv.at[point, side],
+                side,
+            ))
             for side in range(2)
         ]
 
     def send_edges(point):
         pack(edge_out.at[point, 0], errors.at[point], layers - HALO, half)
         pack(edge_out.at[point, 1], errors.at[point], 0, half)
-        for copy in edge_copies(point):
-            copy.start()
+        start(edge_copies(point))
 
     def piece_copies(point):
         return [
-            pltpu.make_async_remote_copy(
-                src_ref=piece_out.at[point, (0, 1, 1, 0)[slot]],
-                dst_ref=piece_in.at[point, slot],
-                send_sem=piece_send.at[point, slot],
-                recv_sem=piece_recv.at[point, slot],
-                device_id=(tme, around[slot]),
-                device_id_type=MESH,
-            )
+            (slot, remote(
+                piece_out.at[point, (0, 1, 1, 0)[slot]],
+                piece_in.at[point, slot],
+                piece_send.at[point, slot],
+                piece_recv.at[point, slot],
+                slot,
+            ))
             for slot in range(4)
         ]
 
     def send_pieces(point):
         pack(piece_out.at[point, 0], ext_a, off, 1)
         pack(piece_out.at[point, 1], ext_a, end - 2, 1)
-        for copy in piece_copies(point):
-            copy.start()
+        start(piece_copies(point))
 
     def receive_pieces(point):
         places = (off - layers, end + layers - 2, 0, end + layers)
-        for slot, copy in enumerate(piece_copies(point)):
-            copy.wait_recv()
+        arrive(piece_copies(point))
+        for slot in range(4):
             unpack(piece_in.at[point, slot], ext_a, places[slot], 1)
 
     def receive_edges(point, place):
-        for side, copy in enumerate(edge_copies(point)):
-            copy.wait_recv()
+        arrive(edge_copies(point))
+        for side in range(2):
             place(side, edge_in.at[point, side])
 
     def pass_residual(point):
@@ -632,13 +654,11 @@
     out_ref[1] = result[DOF:]
 
     guess_copy.wait_send()
-    for copy in tables_copies:
-        copy.wait_send()
+    finish_sends(tables_copies)
 
     for point in range(2):
         for turn in range(2):
-            for copy in state_copies(point, turn) + force_copies(point, turn):
-                copy.wait_send()
+            finish_sends(state_copies(point, turn) + force_copies(point, turn))
     for index in range(2):
         for distance, copy in residual_copies(index):
 
@@ -647,13 +667,11 @@
                 copy.wait_send()
 
     def sweep_done(point, carry):
-        for copy in edge_copies(point):
-            copy.wait_send()
+        finish_sends(edge_copies(point))
 
         @pl.when(point < final - 1)
         def _():
-            for copy in piece_copies(point):
-                copy.wait_send()
+            finish_sends(piece_copies(point))
 
         return carry
 
@@ -687,12 +705,12 @@
             vmem((4 * DOF, 8 * DOF), BF16),
             vmem((ext - 2 * LAYER, 8 * DOF), F32),
             vmem((own, own), BF16),
-            vmem((2, COARSEN, own + 2 * HALO * LAYER, wide), F32),
+            vmem((2, COARSEN, own, wide), F32),
             vmem((2, own, wide), F32),
             vmem((2, ext, wide), F32),
             vmem((ext, wide), F32),
-            vmem((4, ext, wide), BF16),
-            vmem((4, ext, 8 * DOF), F32),
+            vmem((4, 2, LAYER, wide), BF16),
+            vmem((4, 4, LAYER, 4 * DOF), F32),
             vmem((points, own, wide), F32),
             vmem((8, own), F32),
             vmem((4, 8, own), F32),

time: 67.3 us -> 58.4 us (0.87)
  the two profiles are of different devices: /device:TPU:6 before, /device:TPU:134 now
where the time goes in v4:
time: 58.4 us; the launch traced here: 57.8 us
  Pallas kernels  56.2 us (96%)
  other arithmetic  1.63 us (3%)
    pallas_call x1, Pallas kernels, body(): pl.pallas_call(functools.partial(kernel, layers, count), out_shape=jax.Sh...  56.2 us
    add x1, other arithmetic, body(): return guess + errors  1.63 us

profile of v4, /device:TPU:134, one launch (start us, length us, event | category | flops | bytes accessed | tf_op | source)
XLA Modules:
  0.0 57.8 jit_solution(14101416862637397016)
XLA Ops:
  0.0 0.0 copy-start
  0.0 56.2 %shard_map.82 = f32[2,64,384]{2,1,0:T(8,128)} custom-call(f32[64,384]{1,0:T(8,128)} %init_hbm.1, f32[2,64,384]{2,1,0:T(8,128)} %guess_hbm.1, f32[8,64,384]{2,1,0:T(8,128)} %forcing_hbm.1, f32[64,64]{1,0:T(8,128)} %volume_hbm.1, f32[3,64,64]{2,1,0:T(8,128)} %faces_hbm.1, f32[384]{0:T(512)} %scales_hbm.1, s32[384]{0:T(512)} %ids_hbm.1, s32[6,384]{1,0:T(8,128)} %walls_hbm.1), custom_call_target="tpu_custom_call" | custom-call | tf_op jit(solution)/shard_map/pallas_call | solution.py:691
  56.2 0.0 copy-done
  56.2 1.6 %add.3 = f32[2,64,384]{2,1,0:T(8,128)} add(f32[2,64,384]{2,1,0:T(8,128)S(1)} %copy-done, f32[2,64,384]{2,1,0:T(8,128)} %shard_map.82) | non-fusion elementwise | flops 49152 | bytes 589824 | tf_op jit(solution)/shard_map/add | solution.py:761
Async XLA Ops:
  0.0 56.2 %copy-start = (f32[2,64,384]{2,1,0:T(8,128)S(1)}, f32[2,64,384]{2,1,0:T(8,128)}, u32[]{:S(2)}) copy-start(f32[2,64,384]{2,1,0:T(8,128)} %guess_hbm.1) | copy-start | bytes 589828

commit v5 on v4

--- a/solution.py
+++ b/solution.py
@@ -90,6 +90,7 @@
     sources,
     guess_grid,
     exts,
+    ext_a,
     spare,
     split,
     prod,
@@ -107,8 +108,10 @@
     piece_in,
     edge_out,
     edge_in,
-    res_out,
-    res_in,
+    far_out,
+    far_in,
+    rest_out,
+    rest_in,
     load_sem,
     tables_send,
     tables_recv,
@@ -124,15 +127,16 @@
     piece_recv,
     edge_send,
     edge_recv,
-    res_send,
-    res_recv,
+    far_send,
+    far_recv,
+    rest_send,
+    rest_recv,
 ):
     times = lax.axis_size("tm")
     spaces = lax.axis_size("space")
     tme = lax.axis_index("tm")
     sme = lax.axis_index("space")
     own = layers * LAYER
-    ext_a = exts.at[0]
     off = 2 * HALO
     end = off + layers
     around = [lax.rem(sme + spaces + step, spaces) for step in (1, -1, 2, -2)]
@@ -196,7 +200,10 @@
         )
 
     def rows_of(layer, number=1):
-        return pl.ds(layer * LAYER, number * LAYER)
+        first = layer * LAYER
+        if not isinstance(layer, int):
+            first = pl.multiple_of(first, LAYER)
+        return pl.ds(first, number * LAYER)
 
     for copy in loads[:3]:
         copy.wait()
@@ -458,94 +465,48 @@
         whole_step(x, size, off - HALO, end + HALO, finish, keep)
 
     def outer_step(x, size, finish):
-        lower = {layer: split_of(x[here(layer), :]) for layer in range(HALO)}
-        upper = {layer: split_of(x[here(layer), :]) for layer in range(top - HALO, top)}
+        blocks = {
+            layer: split_of(x[here(layer), :])
+            for layer in (*range(HALO), *range(top - HALO, top))
+        }
         for stage in range(4):
-            sides = []
-            for side, blocks in enumerate((lower, upper)):
-                first = stage if side == 0 else top - stage - HALO
-                span = range(first, first + HALO)
-                next_in = first + HALO if side == 0 else first - 1
-                second_in = next_in + 1 if side == 0 else next_in - 1
-                tall = dict(zip(span, products([blocks[layer] for layer in span], 1)))
-                tall[next_in] = prod[stage, 2 * side]
-                tall[second_in] = prod[stage, 2 * side + 1]
-                blocks[next_in] = split[stage, side]
-                inner = range(first + 1, first + 1 + HALO) if side == 0 else range(first - 1, first - 1 + HALO)
-                flat = dict(zip(inner, products([blocks[layer] for layer in inner], 0)))
-                sides.append((inner, flat, tall))
-            lower, upper = [
-                advance(x, size, stage, inner, flat, tall, finish) for inner, flat, tall in sides
-            ]
+            low, high = stage, top - stage - HALO
+            span = (*range(low, low + HALO), *range(high, high + HALO))
+            inner = (*range(low + 1, low + 1 + HALO), *range(high - 1, high - 1 + HALO))
+            tall = dict(zip(span, products([blocks[layer] for layer in span], 1)))
+            for place, layer in enumerate((low + HALO, low + HALO + 1, high - 1, high - 2)):
+                tall[layer] = prod[stage, place]
+            blocks[low + HALO] = split[stage, 0]
+            blocks[high - 1] = split[stage, 1]
+            flat = dict(zip(inner, products([blocks[layer] for layer in inner], 0)))
+            blocks = advance(x, size, stage, inner, flat, tall, finish)
+
+    core = lax.rem(sme, 2)
+    far_first = core * (layers - HALO)
+    rest_first = (1 - core) * HALO
 
     def residual_copies(index):
         point = count * tme + index
         result = []
         for step in range(times - 1, 0, -1):
-            result.append((
-                step,
-                pltpu.make_async_remote_copy(
-                    src_ref=res_out.at[index],
-                    dst_ref=res_in.at[point],
-                    send_sem=res_send.at[index, step],
-                    recv_sem=res_recv.at[point],
-                    device_id=(lax.rem(tme + step, times), sme),
-                    device_id_type=MESH,
-                ),
-            ))
+            for source, target, send, recv in (
+                (far_out, far_in, far_send, far_recv),
+                (rest_out, rest_in, rest_send, rest_recv),
+            ):
+                result.append((
+                    step,
+                    pltpu.make_async_remote_copy(
+                        src_ref=source.at[index],
+                        dst_ref=target.at[point],
+                        send_sem=send.at[index, step],
+                        recv_sem=recv.at[point],
+                        device_id=(lax.rem(tme + step, times), sme),
+                        device_id_type=MESH,
+                    ),
+                ))
         return result
 
-    def fine(index, carry):
-        turn = index // 2
-        point = lax.rem(index + jnp.minimum(tme, 1), 2)
-        ext = exts.at[point]
-        receive_state(point, turn)
-
-        def finish(step):
-            def store(layer, value):
-                if off <= layer < end:
-                    value = value + sources[point, 2 * turn + step, rows_of(layer - off), :]
-                ext[rows_of(layer), :] = value
-
-            return store
-
-        whole_step(ext, 1.0, off - 2 * HALO, end + 2 * HALO, finish(0))
-        add_force(point, turn)
-        inner_step(ext, 1.0, finish(1), keep=False)
-
-        @pl.when(turn == 0)
-        def _():
-            send_state(point, 1)
-
-        @pl.when(turn == 1)
-        def _():
-            place = count * tme + point
-            errors[place] = ext[rows_of(off, layers), :] - guess_grid[point]
-            pack(res_out.at[point], errors.at[place], 0, layers // 2)
-            for distance, copy in residual_copies(point):
-
-                @pl.when(tme + distance < times)
-                def _():
-                    copy.start()
-
-        return carry
-
-    lax.fori_loop(0, 4, fine, 0)
-
     final = count * tme + count - 1
-
-    def take_residual(point):
-        @pl.when(point < count * tme)
-        def _():
-            pltpu.make_async_remote_copy(
-                src_ref=res_out.at[0],
-                dst_ref=res_in.at[point],
-                send_sem=res_send.at[0, 0],
-                recv_sem=res_recv.at[point],
-                device_id=(lax.rem(tme + 1, times), sme),
-                device_id_type=MESH,
-            ).wait_recv()
-            unpack(res_in.at[point], errors.at[point], 0, layers // 2)
 
     def edge_copies(point):
         return [
@@ -559,10 +520,19 @@
             for side in range(2)
         ]
 
-    def send_edges(point):
-        pack(edge_out.at[point, 0], errors.at[point], layers - HALO, half)
-        pack(edge_out.at[point, 1], errors.at[point], 0, half)
-        start(edge_copies(point))
+    def send_edge(point, side):
+        pack(edge_out.at[point, side], errors.at[point], layers - HALO if side == 0 else 0, half)
+        start(edge_copies(point)[side : side + 1])
+
+    def landed(source, target, send, recv, point):
+        pltpu.make_async_remote_copy(
+            src_ref=source.at[0],
+            dst_ref=target.at[point],
+            send_sem=send.at[0, 0],
+            recv_sem=recv.at[point],
+            device_id=(lax.rem(tme + 1, times), sme),
+            device_id_type=MESH,
+        ).wait_recv()
 
     def piece_copies(point):
         return [
@@ -593,23 +563,93 @@
             place(side, edge_in.at[point, side])
 
     def pass_residual(point):
-        @pl.when(point <= final)
-        def _():
-            take_residual(point)
-
-        @pl.when(point < final)
-        def _():
-            send_edges(point)
-
-    pass_residual(0)
-    ext_a[rows_of(off, layers), :] = errors[0]
-
-    @pl.when(final > 1)
+        passed = point < final
+        foreign = point < count * tme
+
+        @pl.when(jnp.logical_and(point <= final, foreign))
+        def _():
+            landed(far_out, far_in, far_send, far_recv, point)
+            for side in range(2):
+
+                @pl.when(jnp.logical_and(passed, core == 1 - side))
+                def _():
+                    start([(side, remote(
+                        far_in.at[point],
+                        edge_in.at[point, side],
+                        edge_send.at[point, side],
+                        edge_recv.at[point, side],
+                        side,
+                    ))])
+
+            landed(rest_out, rest_in, rest_send, rest_recv, point)
+            unpack(far_in.at[point], errors.at[point], far_first, half)
+            unpack(rest_in.at[point], errors.at[point], rest_first, 1)
+            for side in range(2):
+
+                @pl.when(jnp.logical_and(passed, core == side))
+                def _():
+                    send_edge(point, side)
+
+        @pl.when(jnp.logical_and(passed, jnp.logical_not(foreign)))
+        def _():
+            for side in range(2):
+                send_edge(point, side)
+
+    def begin_sweep():
+        pass_residual(0)
+        ext_a[rows_of(off, layers), :] = errors[0]
+
+        @pl.when(final > 1)
+        def _():
+            send_pieces(0)
+
+    def fine(index, carry):
+        @pl.when(jnp.logical_and(index == 3, tme == times - 1))
+        def _():
+            begin_sweep()
+
+        turn = index // 2
+        point = lax.rem(index + jnp.minimum(tme, 1), 2)
+        ext = exts.at[point]
+        receive_state(point, turn)
+
+        def finish(step):
+            def store(layer, value):
+                if off <= layer < end:
+                    value = value + sources[point, 2 * turn + step, rows_of(layer - off), :]
+                ext[rows_of(layer), :] = value
+
+            return store
+
+        whole_step(ext, 1.0, off - 2 * HALO, end + 2 * HALO, finish(0))
+        add_force(point, turn)
+        inner_step(ext, 1.0, finish(1), keep=False)
+
+        @pl.when(turn == 0)
+        def _():
+            send_state(point, 1)
+
+        @pl.when(turn == 1)
+        def _():
+            place = count * tme + point
+            errors[place] = ext[rows_of(off, layers), :] - guess_grid[point]
+            pack(far_out.at[point], errors.at[place], far_first, half)
+            pack(rest_out.at[point], errors.at[place], rest_first, 1)
+            for distance, copy in residual_copies(point):
+
+                @pl.when(tme + distance < times)
+                def _():
+                    copy.start()
+
+        return carry
+
+    lax.fori_loop(0, 4, fine, 0)
+
+    @pl.when(tme < times - 1)
     def _():
-        send_pieces(0)
+        begin_sweep()
 
     pass_residual(1)
-    pass_residual(2)
 
     receive_edges(0, lambda side, ref: unpack(ref, ext_a, off - HALO if side == 0 else end, half))
 
@@ -626,14 +666,18 @@
         def _():
             send_pieces(point)
 
+        @pl.when(point == 1)
+        def _():
+            pass_residual(2)
+
         pass_residual(point + 2)
 
         @pl.when(point < final)
         def _():
-            receive_pieces(point - 1)
             receive_edges(
                 point, lambda side, ref: unpack(ref, spare, off - HALO if side == 0 else end, half)
             )
+            receive_pieces(point - 1)
 
             def finish_outer(layer, value):
                 ext_a[rows_of(layer), :] = value + spare[rows_of(layer), :]
@@ -647,9 +691,9 @@
     packed = jnp.where(left_lanes(own), errors[final - 1], errors[final])
     parts = [
         lax.dot_general(part, perm_ref[...], (((0,), (0,)), ((), ())), preferred_element_type=F32)
-        for part in thirds(packed)
+        for part in halves(packed)
     ]
-    result = (parts[0] + parts[1]) + parts[2]
+    result = parts[0] + parts[1]
     out_ref[0] = result[:DOF]
     out_ref[1] = result[DOF:]
 
@@ -709,6 +753,7 @@
             vmem((2, own, wide), F32),
             vmem((2, ext, wide), F32),
             vmem((ext, wide), F32),
+            vmem((ext, wide), F32),
             vmem((4, 2, LAYER, wide), BF16),
             vmem((4, 4, LAYER, 4 * DOF), F32),
             vmem((points, own, wide), F32),
@@ -725,8 +770,10 @@
             vmem((points, 4, LAYER, wide), F32),
             vmem((points, 2, HALO // 2 * LAYER, wide), F32),
             vmem((points, 2, HALO // 2 * LAYER, wide), F32),
-            vmem((2, own // 2, wide), F32),
-            vmem((points, own // 2, wide), F32),
+            vmem((2, HALO // 2 * LAYER, wide), F32),
+            vmem((points, HALO // 2 * LAYER, wide), F32),
+            vmem((2, LAYER, wide), F32),
+            vmem((points, LAYER, wide), F32),
             dma((8,)),
             dma((4,)),
             dma((4,)),
@@ -744,19 +791,26 @@
             dma((points, 2)),
             dma((2, times)),
             dma((points,)),
+            dma((2, times)),
+            dma((points,)),
         ],
         compiler_params=pltpu.CompilerParams(
-            collective_id=0, has_side_effects=True, vmem_limit_bytes=56 * 1024 * 1024
+            collective_id=0, has_side_effects=True, vmem_limit_bytes=40 * 1024 * 1024
         ),
     )(
-        init_state,
-        guess,
-        forcing,
-        volume_block,
-        face_blocks,
-        elem_scales,
-        element_ids,
-        walls,
+        *(
+            pltpu.with_memory_space_constraint(field, pltpu.HBM)
+            for field in (
+                init_state,
+                guess,
+                forcing,
+                volume_block,
+                face_blocks,
+                elem_scales,
+                element_ids,
+                walls,
+            )
+        )
     )
     return guess + errors
 

time: 58.4 us -> 56.7 us (0.971)
  other arithmetic: 1.63 us -> 0.7 us
    add x1, other arithmetic: 1.63 us -> 0.7 us  [body(): return guess + errors]
where the time goes in v5:
time: 56.7 us; the launch traced here: 56.6 us
  Pallas kernels  55.9 us (99%)
  other arithmetic  0.7 us (1%)
    pallas_call x1, Pallas kernels, body(): pl.pallas_call(functools.partial(kernel, layers, count), out_shape=jax.Sh...  55.9 us

profile of v5, /device:TPU:134, one launch (start us, length us, event | category | flops | bytes accessed | tf_op | source)
XLA Modules:
  0.0 56.6 jit_solution(10483997122152299010)
XLA Ops:
  0.0 0.0 copy-start
  0.0 55.9 %shard_map.82 = f32[2,64,384]{2,1,0:T(8,128)S(1)} custom-call(f32[64,384]{1,0:T(8,128)} %init_hbm.1, f32[2,64,384]{2,1,0:T(8,128)} %guess_hbm.1, f32[8,64,384]{2,1,0:T(8,128)} %forcing_hbm.1, f32[64,64]{1,0:T(8,128)} %volume_hbm.1, f32[3,64,64]{2,1,0:T(8,128)} %faces_hbm.1, f32[384]{0:T(512)} %scales_hbm.1, s32[384]{0:T(512)} %ids_hbm.1, s32[6,384]{1,0:T(8,128)} %walls_hbm.1), custom_call_target="tpu_custom_call" | custom-call | tf_op jit(solution)/shard_map/pallas_call | solution.py:735
  55.9 0.0 copy-done
  55.9 0.7 %add.3 = f32[2,64,384]{2,1,0:T(8,128)} add(f32[2,64,384]{2,1,0:T(8,128)S(1)} %copy-done, f32[2,64,384]{2,1,0:T(8,128)S(1)} %shard_map.82) | non-fusion elementwise | flops 49152 | bytes 589824 | tf_op jit(solution)/shard_map/add | solution.py:815
Async XLA Ops:
  0.0 55.9 %copy-start = (f32[2,64,384]{2,1,0:T(8,128)S(1)}, f32[2,64,384]{2,1,0:T(8,128)}, u32[]{:S(2)}) copy-start(f32[2,64,384]{2,1,0:T(8,128)} %guess_hbm.1) | copy-start | bytes 589828

commit v6 on v5

--- a/solution.py
+++ b/solution.py
@@ -35,6 +35,11 @@
 def select_rows(perm, values):
     hi, mid, lo = thirds(values)
     return (times_t(perm, hi) + times_t(perm, mid)) + times_t(perm, lo)
+
+
+def select_rows_16(perm, values):
+    high, low = halves(values)
+    return times_t(perm, high) + times_t(perm, low)
 
 
 def left_lanes(rows):
@@ -91,7 +96,6 @@
     guess_grid,
     exts,
     ext_a,
-    spare,
     split,
     prod,
     errors,
@@ -184,9 +188,6 @@
         (forcing_hbm, forcing_ref),
     )
     loads = [pltpu.make_async_copy(a, b, load_sem.at[i]) for i, (a, b) in enumerate(pairs)]
-    for copy in loads:
-        copy.start()
-
     barrier = pltpu.get_barrier_semaphore()
     for slot in range(4):
 
@@ -198,6 +199,9 @@
         pl.semaphore_signal(
             barrier, inc=1, device_id=(lax.rem(tme + step, times), sme), device_id_type=MESH
         )
+
+    for copy in loads:
+        copy.start()
 
     def rows_of(layer, number=1):
         first = layer * LAYER
@@ -215,7 +219,7 @@
     perm_ref[...] = perm
 
     def permuted_pair(first, second):
-        return doubled(select_rows(perm_ref[...], jnp.concatenate([first, second], axis=0)))
+        return doubled(select_rows_16(perm_ref[...], jnp.concatenate([first, second], axis=0)))
 
     loads[3].wait()
     one, two = permuted_pair(guess_ref[0], guess_ref[1])
@@ -316,10 +320,12 @@
     for copy in loads[4:7]:
         copy.wait()
 
+    def permuted(field):
+        return select_rows_16(perm_ref[...], jnp.concatenate([field, field], axis=0))
+
     @pl.when(tme == 0)
     def _():
-        one, _ = permuted_pair(init_ref[...], init_ref[...])
-        exts[0, rows_of(off, layers), :] = one
+        exts[0, rows_of(off, layers), :] = permuted(init_ref[...])
 
     pl.semaphore_wait(barrier, times - 1 + sum(here.astype(jnp.int32) for here in heard))
 
@@ -388,8 +394,7 @@
 
     @pl.when(tme > 0)
     def _():
-        one, _ = permuted_pair(guess_in[...], guess_in[...])
-        exts[0, rows_of(off, layers), :] = one
+        exts[0, rows_of(off, layers), :] = permuted(guess_in[...])
         send_state(0, 0)
 
     send_force(1, 1)
@@ -557,6 +562,13 @@
         for slot in range(4):
             unpack(piece_in.at[point, slot], ext_a, places[slot], 1)
 
+    def unpack_add(source, first):
+        for layer in range(half):
+            one, two = doubled(source[layer * LAYER : (layer + 1) * LAYER, :])
+            low, high = rows_of(first + layer), rows_of(first + half + layer)
+            ext_a[low, :] = ext_a[low, :] + one
+            ext_a[high, :] = ext_a[high, :] + two
+
     def receive_edges(point, place):
         arrive(edge_copies(point))
         for side in range(2):
@@ -604,10 +616,6 @@
             send_pieces(0)
 
     def fine(index, carry):
-        @pl.when(jnp.logical_and(index == 3, tme == times - 1))
-        def _():
-            begin_sweep()
-
         turn = index // 2
         point = lax.rem(index + jnp.minimum(tme, 1), 2)
         ext = exts.at[point]
@@ -645,10 +653,7 @@
 
     lax.fori_loop(0, 4, fine, 0)
 
-    @pl.when(tme < times - 1)
-    def _():
-        begin_sweep()
-
+    begin_sweep()
     pass_residual(1)
 
     receive_edges(0, lambda side, ref: unpack(ref, ext_a, off - HALO if side == 0 else end, half))
@@ -670,30 +675,31 @@
         def _():
             pass_residual(2)
 
+        @pl.when(point < final)
+        def _():
+            receive_pieces(point - 1)
+
+            def finish_outer(layer, value):
+                ext_a[rows_of(layer), :] = value
+
+            outer_step(ext_a, float(COARSEN), finish_outer)
+            receive_edges(
+                point, lambda side, ref: unpack_add(ref, off - HALO if side == 0 else end)
+            )
+
         pass_residual(point + 2)
-
-        @pl.when(point < final)
-        def _():
-            receive_edges(
-                point, lambda side, ref: unpack(ref, spare, off - HALO if side == 0 else end, half)
-            )
-            receive_pieces(point - 1)
-
-            def finish_outer(layer, value):
-                ext_a[rows_of(layer), :] = value + spare[rows_of(layer), :]
-
-            outer_step(ext_a, float(COARSEN), finish_outer)
-
         return carry
 
     lax.fori_loop(1, final + 1, coarse, 0)
 
     packed = jnp.where(left_lanes(own), errors[final - 1], errors[final])
-    parts = [
-        lax.dot_general(part, perm_ref[...], (((0,), (0,)), ((), ())), preferred_element_type=F32)
-        for part in halves(packed)
-    ]
-    result = parts[0] + parts[1]
+    parts = lax.dot_general(
+        jnp.concatenate(halves(packed), axis=1),
+        perm_ref[...],
+        (((0,), (0,)), ((), ())),
+        preferred_element_type=F32,
+    )
+    result = parts[: 2 * DOF] + parts[2 * DOF :]
     out_ref[0] = result[:DOF]
     out_ref[1] = result[DOF:]
 
@@ -752,7 +758,6 @@
             vmem((2, COARSEN, own, wide), F32),
             vmem((2, own, wide), F32),
             vmem((2, ext, wide), F32),
-            vmem((ext, wide), F32),
             vmem((ext, wide), F32),
             vmem((4, 2, LAYER, wide), BF16),
             vmem((4, 4, LAYER, 4 * DOF), F32),

time: 56.7 us -> 56.7 us (level)
  no operation moved by 1% of the time
where the time goes in v6:
time: 56.7 us; the launch traced here: 56.5 us
  Pallas kernels  55.8 us (98%)
  other arithmetic  0.7 us (1%)
    pallas_call x1, Pallas kernels, body(): pl.pallas_call(functools.partial(kernel, layers, count), out_shape=jax.Sh...  55.8 us

profile of v6, /device:TPU:134, one launch (start us, length us, event | category | flops | bytes accessed | tf_op | source)
XLA Modules:
  0.0 56.5 jit_solution(11630942697031557114)
XLA Ops:
  0.0 0.0 copy-start
  0.0 55.8 %shard_map.82 = f32[2,64,384]{2,1,0:T(8,128)S(1)} custom-call(f32[64,384]{1,0:T(8,128)} %init_hbm.1, f32[2,64,384]{2,1,0:T(8,128)} %guess_hbm.1, f32[8,64,384]{2,1,0:T(8,128)} %forcing_hbm.1, f32[64,64]{1,0:T(8,128)} %volume_hbm.1, f32[3,64,64]{2,1,0:T(8,128)} %faces_hbm.1, f32[384]{0:T(512)} %scales_hbm.1, s32[384]{0:T(512)} %ids_hbm.1, s32[6,384]{1,0:T(8,128)} %walls_hbm.1), custom_call_target="tpu_custom_call" | custom-call | tf_op jit(solution)/shard_map/pallas_call | solution.py:741
  55.8 0.0 copy-done
  55.8 0.7 %add.3 = f32[2,64,384]{2,1,0:T(8,128)} add(f32[2,64,384]{2,1,0:T(8,128)S(1)} %copy-done, f32[2,64,384]{2,1,0:T(8,128)S(1)} %shard_map.82) | non-fusion elementwise | flops 49152 | bytes 589824 | tf_op jit(solution)/shard_map/add | solution.py:820
Async XLA Ops:
  0.0 55.8 %copy-start = (f32[2,64,384]{2,1,0:T(8,128)S(1)}, f32[2,64,384]{2,1,0:T(8,128)}, u32[]{:S(2)}) copy-start(f32[2,64,384]{2,1,0:T(8,128)} %guess_hbm.1) | copy-start | bytes 589828

commit v7 on v5

--- a/solution.py
+++ b/solution.py
@@ -273,16 +273,21 @@
 
     def send_state(point, turn):
         ext = exts.at[point]
+        copies = state_copies(point, turn)
         pack(block_out.at[point, turn], ext, off, layers // 2)
+        start(copies[:2])
         pack(strip_out.at[point, turn, 0], ext, end - 2, 1)
         pack(strip_out.at[point, turn, 1], ext, off, 1)
-        start(state_copies(point, turn))
+        start(copies[2:])
 
     def receive_state(point, turn):
         ext = exts.at[point]
-        arrive(state_copies(point, turn))
+        copies = state_copies(point, turn)
+        arrive(copies[:1])
         unpack(block_in.at[point, turn, 0], ext, off - layers, layers // 2)
+        arrive(copies[1:2])
         unpack(block_in.at[point, turn, 1], ext, end, layers // 2)
+        arrive(copies[2:])
         unpack(strip_in.at[point, turn, 0], ext, off - layers - 2, 1)
         unpack(strip_in.at[point, turn, 1], ext, end + layers, 1)
 
@@ -547,9 +552,11 @@
         ]
 
     def send_pieces(point):
+        copies = piece_copies(point)
+        pack(piece_out.at[point, 1], ext_a, end - 2, 1)
+        start(copies[1:3])
         pack(piece_out.at[point, 0], ext_a, off, 1)
-        pack(piece_out.at[point, 1], ext_a, end - 2, 1)
-        start(piece_copies(point))
+        start([copies[0], copies[3]])
 
     def receive_pieces(point):
         places = (off - layers, end + layers - 2, 0, end + layers)

time: 56.7 us -> 57.2 us (level)
  no operation moved by 1% of the time
where the time goes in v7:
time: 57.2 us; the launch traced here: 56.9 us
  Pallas kernels  56.2 us (98%)
  other arithmetic  0.7 us (1%)
    pallas_call x1, Pallas kernels, body(): pl.pallas_call(functools.partial(kernel, layers, count), out_shape=jax.Sh...  56.2 us

profile of v7, /device:TPU:134, one launch (start us, length us, event | category | flops | bytes accessed | tf_op | source)
XLA Modules:
  0.0 56.9 jit_solution(4320288283165197266)
XLA Ops:
  0.0 0.0 copy-start
  0.0 56.2 %shard_map.82 = f32[2,64,384]{2,1,0:T(8,128)S(1)} custom-call(f32[64,384]{1,0:T(8,128)} %init_hbm.1, f32[2,64,384]{2,1,0:T(8,128)} %guess_hbm.1, f32[8,64,384]{2,1,0:T(8,128)} %forcing_hbm.1, f32[64,64]{1,0:T(8,128)} %volume_hbm.1, f32[3,64,64]{2,1,0:T(8,128)} %faces_hbm.1, f32[384]{0:T(512)} %scales_hbm.1, s32[384]{0:T(512)} %ids_hbm.1, s32[6,384]{1,0:T(8,128)} %walls_hbm.1), custom_call_target="tpu_custom_call" | custom-call | tf_op jit(solution)/shard_map/pallas_call | solution.py:742
  56.2 0.0 copy-done
  56.2 0.7 %add.3 = f32[2,64,384]{2,1,0:T(8,128)} add(f32[2,64,384]{2,1,0:T(8,128)S(1)} %copy-done, f32[2,64,384]{2,1,0:T(8,128)S(1)} %shard_map.82) | non-fusion elementwise | flops 49152 | bytes 589824 | tf_op jit(solution)/shard_map/add | solution.py:822
Async XLA Ops:
  0.0 56.2 %copy-start = (f32[2,64,384]{2,1,0:T(8,128)S(1)}, f32[2,64,384]{2,1,0:T(8,128)}, u32[]{:S(2)}) copy-start(f32[2,64,384]{2,1,0:T(8,128)} %guess_hbm.1) | copy-start | bytes 589828
